TPU v7x, 32 devices: a whole 2x2x4 slice. The times are simulated.
32 devices in a mesh: clip: 16 (over z, y, x), frame: 2 (over core).
Axes of the slice: x: 2, y: 2, z: 4, core: 2. Of those that a mesh axis runs over, the one named last changes fastest.
Arguments:
- clip_tokens: bfloat16 [16, 8, 196, 768], P('clip', 'frame'), may hold values from -6 to 6
- clip_class: bfloat16 [16, 768], P('clip'), may hold values from -6 to 6
- output_grad: bfloat16 [16, 8, 196, 768], P('clip', 'frame'), may hold values from -6 to 6
- class_grad: bfloat16 [16, 768], P('clip'), may hold values from -6 to 6
- clip_count: int32 [16], P('clip'), may hold values from 1 to 1, as said below
- time_qkv: bfloat16 [768, 2304], P(('clip', 'frame')), may hold values from -0.21875 to 0.21875
- time_proj: bfloat16 [768, 768], P(('clip', 'frame')), may hold values from -0.625 to 0.625
- time_vec: bfloat16 [5, 768], P(None, ('clip', 'frame'))
- space_qkv: bfloat16 [768, 2304], P(('clip', 'frame')), may hold values from -0.21875 to 0.21875
- space_proj: bfloat16 [768, 768], P(('clip', 'frame')), may hold values from -1.25 to 1.25
- space_vec: bfloat16 [5, 768], P(None, ('clip', 'frame'))
- mlp_up: bfloat16 [768, 3072], P(('clip', 'frame')), may hold values from -0.21875 to 0.21875
- mlp_down: bfloat16 [3072, 768], P(('clip', 'frame')), may hold values from -0.109375 to 0.109375
- mlp_vec: bfloat16 [3, 768], P(None, ('clip', 'frame'))
- mlp_bias: bfloat16 [3072], P(('clip', 'frame')), may hold values from -3 to 3
Outputs:
- block_out: bfloat16 [16, 8, 196, 768], P('clip', 'frame')
- class_out: bfloat16 [16, 768], P('clip')
- token_grad: float32 [16, 8, 196, 768], P('clip', 'frame')
- class_in_grad: float32 [16, 768], P('clip')
- grad_time_qkv: float32 [768, 2304], P(('clip', 'frame'))
- grad_time_proj: float32 [768, 768], P(('clip', 'frame'))
- grad_time_vec: float32 [5, 768], P(None, ('clip', 'frame'))
- grad_space_qkv: float32 [768, 2304], P(('clip', 'frame'))
- grad_space_proj: float32 [768, 768], P(('clip', 'frame'))
- grad_space_vec: float32 [5, 768], P(None, ('clip', 'frame'))
- grad_mlp_up: float32 [768, 3072], P(('clip', 'frame'))
- grad_mlp_down: float32 [3072, 768], P(('clip', 'frame'))
- grad_mlp_vec: float32 [3, 768], P(None, ('clip', 'frame'))
- grad_mlp_bias: float32 [3072], P(('clip', 'frame'))
Inputs may be any that keep to these rules, and one draw needn't show every extreme that they name: Clip slot s of index i of clip is live when s < clip_count[i]; with one slot per index, every clip_count is 1 and every slot is live.
All inputs are finite; a program needn't handle non-finite values.
Results may differ from a plain program's by a relative error of at most 0.015.
Values may be sent and summed in bfloat16 or wider, within the bound.
No kernel may reach another device: no remote copies, remote signals or barrier semaphores. Data moves between devices by JAX's collectives and lax.ppermute only.
A program may use at most 192 MiB of HBM per device.

v0:
```python
import functools

import jax
import jax.numpy as jnp
from jax import lax
from jax.experimental import pallas as pl
from jax.experimental.pallas import tpu as pltpu
from jax.sharding import PartitionSpec as P

HEAD_DIM = 64
EPSILON = 1e-06
FLOAT = jnp.float32
BRAIN = jnp.bfloat16
LANES = 128
BLOCKS = 16
VMEM_BYTES = 56 * 1024 * 1024


def nn(left, right):
    return lax.dot_general(left, right, (((1,), (0,)), ((), ())), preferred_element_type=FLOAT)


def nt(left, right):
    return lax.dot_general(left, right, (((1,), (1,)), ((), ())), preferred_element_type=FLOAT)


def tn(left, right):
    return lax.dot_general(left, right, (((0,), (0,)), ((), ())), preferred_element_type=FLOAT)


def unit_of(values):
    average = jnp.mean(values, axis=-1, keepdims=True)
    centred = values - average
    spread = jnp.mean(centred * centred, axis=-1, keepdims=True)
    inverse = lax.rsqrt(spread + EPSILON)
    return centred * inverse, inverse


def norm_back(unit, inverse, gain, upstream):
    scaled = upstream * gain
    inner = jnp.mean(scaled, axis=-1, keepdims=True)
    along = jnp.mean(scaled * unit, axis=-1, keepdims=True)
    return inverse * (scaled - inner - unit * along)


def column_sum(values):
    return jnp.sum(values, axis=0, keepdims=True)


def row_index(shape):
    return lax.broadcasted_iota(jnp.int32, shape, 0)


def head_map(width):
    lane = lax.broadcasted_iota(jnp.int32, (width, LANES), 0) // HEAD_DIM
    head = lax.broadcasted_iota(jnp.int32, (width, LANES), 1)
    return (lane == head).astype(FLOAT).astype(BRAIN)


def head_spread(width):
    head = lax.broadcasted_iota(jnp.int32, (LANES, width), 0)
    lane = lax.broadcasted_iota(jnp.int32, (LANES, width), 1) // HEAD_DIM
    return (lane == head).astype(FLOAT).astype(BRAIN)


def load_columns(core, mine, other, held, sems):
    half = held.shape[1] // 2
    first = pltpu.make_async_copy(
        mine.at[:, :half], held.at[:, pl.ds(pl.multiple_of(core * half, LANES), half)], sems.at[0]
    )
    second = pltpu.make_async_copy(
        other.at[:, :half], held.at[:, pl.ds(pl.multiple_of((1 - core) * half, LANES), half)], sems.at[1]
    )
    first.start()
    second.start()
    return first, second


def load_mlp(core, mine, other, up, down, sems):
    cut = up.shape[2]
    copies = []
    for k, (source, slot) in enumerate(((mine, core), (other, 1 - core))):
        for t in (0, 1):
            copies.append(
                pltpu.make_async_copy(source.at[:, t * cut : (t + 1) * cut], up.at[2 * slot + t], sems.at[3 * k + t])
            )
        copies.append(pltpu.make_async_copy(source.at[:, 2 * cut :], down.at[:, slot], sems.at[3 * k + 2]))
    for copy in copies:
        copy.start()
    return copies


def wait_all(*copies):
    for group in copies:
        for copy in group:
            copy.wait()


def time_mix_kernel(own, info, tokens, vectors, w_mine, w_other, q_out, k_out, v_out, low_out, held, sems):
    step = pl.program_id(0)
    width = tokens.shape[-1]

    @pl.when(step == 0)
    def _():
        wait_all(load_columns(info[0], w_mine, w_other, held, sems))

    unit, _ = unit_of(tokens[0].astype(FLOAT))
    low = (unit * vectors[0:1] + vectors[1:2]).astype(BRAIN)
    k_out[0] = nn(low, held[:, width : 2 * width]).astype(BRAIN)
    v_out[0] = (nn(low, held[:, 2 * width :]) + vectors[3:4]).astype(BRAIN)

    @pl.when(step < own)
    def _():
        queries = (nn(low, held[:, :width]) + vectors[2:3]).astype(BRAIN)
        q_out[0] = queries * jnp.asarray(HEAD_DIM ** (-0.5), BRAIN)
        low_out[0] = low


def attention_kernel(
    places_here, info, tokens, vectors, q_in, k_in, v_in, begin, sw_mine, sw_other,
    prob_out, att_out, after_out, low_out, mixed_out, sprob_out, satt_out, places_out, class_out,
    held, sems,
):
    step = pl.program_id(0)
    frames = k_in.shape[0]
    rows, width = tokens.shape[1:]
    core = info[0]

    @pl.when(step == 0)
    def _():
        wait_all(load_columns(core, sw_mine, sw_other, held, sems))

    mapping = head_map(width)
    spread = head_spread(width)
    queries = q_in[0]
    scores = [nn(queries * k_in[g], mapping) for g in range(frames)]
    top = functools.reduce(jnp.maximum, scores)
    powers = [jnp.exp(s - top) for s in scores]
    scale = 1.0 / sum(powers)
    total = jnp.zeros((rows, width), FLOAT)
    for g in range(frames):
        prob = (powers[g] * scale).astype(BRAIN)
        prob_out[0, g] = prob
        total = total + nn(prob, spread) * v_in[g].astype(FLOAT)
    attended = total.astype(BRAIN)
    att_out[0] = attended
    place = row_index((rows, 1)) < places_here
    base = tokens[0].astype(FLOAT)
    after = jnp.where(place, base + (nn(attended, held[:, 4 * width :]) + vectors[4:5]), base)
    after_out[0] = after
    unit, _ = unit_of(after)
    low = (unit * vectors[5:6] + vectors[6:7]).astype(BRAIN)
    low_out[0] = low
    mixed_out[0, :, :width] = (
        (nn(low, held[:, :width]) + vectors[7:8]).astype(BRAIN) * jnp.asarray(HEAD_DIM ** (-0.5), BRAIN)
    )
    mixed_out[0, :, width : 2 * width] = nn(low, held[:, width : 2 * width]).astype(BRAIN)
    mixed_out[0, :, 2 * width :] = (nn(low, held[:, 2 * width : 3 * width]) + vectors[8:9]).astype(BRAIN)
    lane = lax.broadcasted_iota(jnp.int32, (1, LANES), 1)
    masks = [(lane // HEAD_DIM == e).astype(FLOAT).astype(BRAIN) for e in (0, 1)]
    key_ok = lax.broadcasted_iota(jnp.int32, (1, rows), 1) <= places_here
    for pair in range(width // LANES):
        at = pair * LANES
        q2 = mixed_out[0, :, at : at + LANES]
        k2 = mixed_out[0, :, width + at : width + at + LANES]
        v2 = mixed_out[0, :, 2 * width + at : 2 * width + at + LANES]
        result = []
        for e in (0, 1):
            logits = jnp.where(key_ok, nt(q2 * masks[e], k2), -1e30)
            power = jnp.exp(logits - jnp.max(logits, axis=-1, keepdims=True))
            prob = (power * (1.0 / jnp.sum(power, axis=-1, keepdims=True))).astype(BRAIN)
            sprob_out[0, 2 * pair + e] = prob
            result.append(nn(prob, v2))
        satt_out[0, :, at : at + LANES] = jnp.where(lane < HEAD_DIM, result[0], result[1]).astype(BRAIN)
    spatial = nn(satt_out[0], held[:, 3 * width : 4 * width]) + vectors[9:10]
    places_out[0] = jnp.where(place, after, 0.0) + spatial

    @pl.when(step == 0)
    def _():
        class_out[...] = begin[...]

    class_row = column_sum(jnp.where(row_index((rows, 1)) == places_here, spatial, 0.0))
    class_out[0:1] = class_out[0:1] + class_row


def gelu_parts(values):
    half = 0.5 + 0.5 * lax.erf(values * (0.5 ** 0.5))
    density = jnp.exp(values * values * (-0.5)) * (0.5 / 3.141592653589793) ** 0.5
    return values * half, half + values * density


def mlp_kernel(
    places_here, all_frames, info, alive, places, grads, class_row, class_own, class_far, vectors, bias,
    w_mine, w_other,
    out, low_out, hidden_out, feed_out, before_out, rows_out, sums, slopes, up, down, sems,
):
    step = pl.program_id(0)
    rows, width = places.shape[1:]
    core = info[0]

    @pl.when(step == 0)
    def _():
        sums[...] = jnp.zeros_like(sums)
        wait_all(load_mlp(core, w_mine, w_other, up, down, sems))

    class_mid = class_row[0:1] + (class_own[0:1] + class_far[0:1]) * all_frames ** (-0.5)
    class_at = row_index((rows, 1)) == places_here
    is_class = class_at & (step == pl.num_programs(0) - 1)
    kept = jnp.logical_not(class_at & (info[1] == 0))
    values = jnp.where(is_class, class_mid, places[0])
    unit, inverse = unit_of(values)
    low = (unit * vectors[10:11] + vectors[11:12]).astype(BRAIN)
    low_out[0] = low
    feed = jnp.zeros((rows, width), FLOAT)
    chunks = hidden_out.shape[-1] // width
    per = down.shape[0] // chunks
    for j in range(chunks):
        before = nn(low, up[j].reshape(width, width)) + bias[j : j + 1]
        hidden, slope = gelu_parts(before)
        hidden = hidden.astype(BRAIN)
        hidden_out[0, :, j * width : (j + 1) * width] = hidden
        slopes[j] = slope
        feed = feed + nn(hidden, down[j * per : (j + 1) * per].reshape(width, width))
    out[0] = ((values + (feed + vectors[12:13])) * alive[0]).astype(BRAIN)

    row_grad = grads[0].astype(FLOAT) * alive[0]
    feed_grad = row_grad.astype(BRAIN)
    feed_kept = jnp.where(kept, row_grad, 0.0).astype(BRAIN)
    feed_out[0] = feed_kept
    sums[2:3] = sums[2:3] + column_sum(feed_kept.astype(FLOAT))
    upstream = jnp.zeros((rows, width), FLOAT)
    for j in range(chunks):
        hidden_grad = nt(feed_grad, down[j * per : (j + 1) * per].reshape(width, width))
        before_grad = (hidden_grad * slopes[j]).astype(BRAIN)
        before_kept = jnp.where(kept, before_grad.astype(FLOAT), 0.0)
        before_out[0, :, j * width : (j + 1) * width] = before_kept.astype(BRAIN)
        sums[3 + j : 4 + j] = sums[3 + j : 4 + j] + column_sum(before_kept)
        upstream = upstream + nt(before_grad, up[j].reshape(width, width))
    rows_out[0] = row_grad + norm_back(unit, inverse, vectors[10:11], upstream)
    upstream = jnp.where(kept, upstream, 0.0)
    sums[0:1] = sums[0:1] + column_sum(upstream * unit)
    sums[1:2] = sums[1:2] + column_sum(upstream)


def space_back_kernel(
    places_here, all_frames, info, rows_grad, class_grad, after, mixed, sprob, vectors, begin,
    sw_mine, sw_other,
    branch_out, mixed_out, after_out, time_out, att_out, sums, held, sems,
):
    step = pl.program_id(0)
    rows, width = after.shape[1:]
    core = info[0]

    @pl.when(step == 0)
    def _():
        sums[...] = begin[...]
        wait_all(load_columns(core, sw_mine, sw_other, held, sems))

    index = row_index((rows, 1))
    place = index < places_here
    class_at = index == places_here
    offset = places_here % 16
    share = class_grad[0, offset : offset + 1] * all_frames ** (-0.5)
    direct = jnp.where(place, rows_grad[0], 0.0)
    branch = jnp.where(class_at, share, direct).astype(BRAIN)
    branch_out[0] = branch
    sums[4:5] = sums[4:5] + column_sum(branch.astype(FLOAT))
    att_grad = nt(branch, held[:, 3 * width : 4 * width]).astype(BRAIN)
    lane = lax.broadcasted_iota(jnp.int32, (1, LANES), 1)
    masks = [(lane // HEAD_DIM == e).astype(FLOAT).astype(BRAIN) for e in (0, 1)]
    for pair in range(width // LANES):
        at = pair * LANES
        a2 = att_grad[:, at : at + LANES]
        q2 = mixed[0, :, at : at + LANES]
        k2 = mixed[0, :, width + at : width + at + LANES]
        v2 = mixed[0, :, 2 * width + at : 2 * width + at + LANES]
        queries, key_rows, value_rows = [], [], []
        for e in (0, 1):
            prob = sprob[0, 2 * pair + e]
            wide = prob.astype(FLOAT)
            prob_grad = nt(a2 * masks[e], v2)
            weighted = wide * prob_grad
            rowdot = jnp.sum(weighted, axis=-1, keepdims=True)
            score = (weighted - wide * rowdot).astype(BRAIN)
            queries.append(nn(score, k2))
            key_rows.append(tn(score, q2))
            value_rows.append(tn(prob, a2))
        left = lane < HEAD_DIM
        q_grad = (jnp.where(left, queries[0], queries[1]) * HEAD_DIM ** (-0.5)).astype(BRAIN)
        v_grad = jnp.where(left, value_rows[0], value_rows[1]).astype(BRAIN)
        mixed_out[0, :, at : at + LANES] = q_grad
        mixed_out[0, :, width + at : width + at + LANES] = jnp.where(left, key_rows[0], key_rows[1]).astype(BRAIN)
        mixed_out[0, :, 2 * width + at : 2 * width + at + LANES] = v_grad
    sums[2:3] = sums[2:3] + column_sum(mixed_out[0, :, :width].astype(FLOAT))
    sums[3:4] = sums[3:4] + column_sum(mixed_out[0, :, 2 * width :].astype(FLOAT))
    upstream = nt(mixed_out[0], held[:, : 3 * width])
    unit, inverse = unit_of(after[0])
    inner = norm_back(unit, inverse, vectors[5:6], upstream)
    sums[0:1] = sums[0:1] + column_sum(upstream * unit)
    sums[1:2] = sums[1:2] + column_sum(upstream)
    sums[6:7] = sums[6:7] + column_sum(jnp.where(class_at, inner, 0.0))
    after_grad = jnp.where(place, direct + inner, 0.0)
    after_out[0] = after_grad
    low = after_grad.astype(BRAIN)
    time_out[0] = low
    sums[5:6] = sums[5:6] + column_sum(low.astype(FLOAT))
    att_out[0] = nt(low, held[:, 4 * width :]).astype(BRAIN)


def time_back_kernel(q_in, k_in, v_in, prob_in, att_in, q_out, own_out, far_out):
    own, rows, width = q_in.shape
    frames = k_in.shape[0]
    mapping = head_map(width)
    spread = head_spread(width)
    size = 16

    def chunk(index, carry):
        at = pl.ds(pl.multiple_of(index * size, size), size)
        values = [v_in[g, at] for g in range(frames)]
        att = [att_in[f, at] for f in range(own)]
        products = jnp.concatenate([att[f] * values[g] for f in range(own) for g in range(frames)], axis=0)
        prob_grad = nn(products, mapping)
        probs = [prob_in[f, g, at] for f in range(own) for g in range(frames)]
        scores = []
        for f in range(own):
            wide = [probs[f * frames + g].astype(FLOAT) for g in range(frames)]
            weighted = [
                wide[g] * prob_grad[(f * frames + g) * size : (f * frames + g + 1) * size] for g in range(frames)
            ]
            rowdot = sum(weighted)
            scores += [(weighted[g] - wide[g] * rowdot).astype(BRAIN) for g in range(frames)]
        score_wide = nn(jnp.concatenate(scores, axis=0), spread)
        prob_wide = nn(jnp.concatenate(probs, axis=0), spread)

        def part(array, f, g):
            return array[(f * frames + g) * size : (f * frames + g + 1) * size]

        for f in range(own):
            total = sum(part(score_wide, f, g) * k_in[g, at].astype(FLOAT) for g in range(frames))
            q_out[f, at] = (total * HEAD_DIM ** (-0.5)).astype(BRAIN)
        queries = [q_in[f, at].astype(FLOAT) for f in range(own)]
        wide_att = [a.astype(FLOAT) for a in att]
        for g in range(frames):
            key_grad = sum(part(score_wide, f, g) * queries[f] for f in range(own)).astype(BRAIN)
            value_grad = sum(part(prob_wide, f, g) * wide_att[f] for f in range(own)).astype(BRAIN)
            if g < own:
                own_out[0, g, at] = key_grad
                own_out[1, g, at] = value_grad
            else:
                far_out[0, g - own, at] = key_grad
                far_out[1, g - own, at] = value_grad
        return carry

    lax.fori_loop(0, rows // size, chunk, 0)


def time_mix_back_kernel(info, tokens, vectors, mixed, after_grad, w_mine, w_other, token_out, sums, held, sems):
    step = pl.program_id(0)
    width = tokens.shape[-1]

    @pl.when(step == 0)
    def _():
        sums[...] = jnp.zeros_like(sums)
        wait_all(load_columns(info[0], w_mine, w_other, held, sems))

    sums[2:3] = sums[2:3] + column_sum(mixed[0, :, :width].astype(FLOAT))
    sums[3:4] = sums[3:4] + column_sum(mixed[0, :, 2 * width :].astype(FLOAT))
    upstream = nt(mixed[0], held[...])
    unit, inverse = unit_of(tokens[0].astype(FLOAT))
    token_out[0] = after_grad[0] + norm_back(unit, inverse, vectors[0:1], upstream)
    sums[0:1] = sums[0:1] + column_sum(upstream * unit)
    sums[1:2] = sums[1:2] + column_sum(upstream)


def time_outer_kernel(info, left, right, sums, out):
    half = right.shape[1]
    out[:, :half] = tn(left[...], right[...]).astype(BRAIN)
    out[:, half:] = sums[...].astype(BRAIN)


def space_outer_kernel(info, low, mixed, att, branch, time_att, time_grad, out):
    width = low.shape[1]
    half = out.shape[1]
    rest = 3 * width - half

    @pl.when(info[0] == 0)
    def _():
        out[...] = tn(low[...], mixed[:, :half]).astype(BRAIN)

    @pl.when(info[0] == 1)
    def _():
        out[:, :rest] = tn(low[...], mixed[:, half:]).astype(BRAIN)
        out[:, rest : rest + width] = tn(att[...], branch[...]).astype(BRAIN)
        out[:, rest + width :] = tn(time_att[...], time_grad[...]).astype(BRAIN)


def mlp_outer_kernel(info, low, before, hidden, feed, mine, other):
    step = pl.program_id(0)
    blocks, total, width = mine.shape
    cut = total // 4
    per = blocks // pl.num_programs(0)
    part = tn(low[...], before[...]).astype(BRAIN).reshape(blocks, cut, width)
    at = pl.ds(pl.multiple_of((step % 2) * cut, 16), cut)
    is_mine = step // 2 == info[0]

    @pl.when(is_mine)
    def _():
        mine[:, at] = part

    @pl.when(jnp.logical_not(is_mine))
    def _():
        other[:, at] = part

    value = tn(hidden[...], feed[...]).astype(BRAIN).reshape(per, 2, 2 * cut, width)
    first = info[0] == 0
    rows = pl.ds(pl.multiple_of(step * per, per), per)
    mine[rows, 2 * cut :] = jnp.where(first, value[:, 0], value[:, 1])
    other[rows, 2 * cut :] = jnp.where(first, value[:, 1], value[:, 0])


def smem():
    return pl.BlockSpec(memory_space=pltpu.SMEM)


def hbm():
    return pl.BlockSpec(memory_space=pl.ANY)


def whole(shape):
    return pl.BlockSpec(shape, lambda *_: (0,) * len(shape))


def per_frame(shape, first=0):
    return pl.BlockSpec((1,) + shape[1:], lambda s: (s + first,) + (0,) * (len(shape) - 1))


def sds(shape, kind):
    return jax.ShapeDtypeStruct(shape, kind)


def call(kernel, grid, inputs, outputs, scratch=(), flops=0, nbytes=0, deps=(), previous=(), prefetch=0):
    count = len(inputs)
    skip = len(previous) + len(deps)

    def inner(*refs):
        kernel(*refs[:count], *refs[count + skip :])

    specs = [spec for spec, _ in inputs[prefetch:]] + [hbm()] * skip
    common = dict(
        out_shape=[shape for _, shape in outputs],
        compiler_params=pltpu.CompilerParams(vmem_limit_bytes=VMEM_BYTES),
        input_output_aliases={count + n: n for n in range(len(previous))},
        cost_estimate=pl.CostEstimate(flops=1, bytes_accessed=1, transcendentals=0),
    )
    places = dict(grid=grid, in_specs=specs, out_specs=[spec for spec, _ in outputs], scratch_shapes=list(scratch))
    if prefetch:
        common["grid_spec"] = pltpu.PrefetchScalarGridSpec(num_scalar_prefetch=prefetch, **places)
    else:
        common.update(places)
    return pl.pallas_call(inner, **common)(*[array for _, array in inputs], *previous, *deps)


def time_outer(slot, left, right, sums, deps=()):
    rows, width = left.shape
    half = right.shape[1] // 2
    shape = (width, half + sums.shape[1])
    return call(
        time_outer_kernel, (1,),
        [
            (None, slot),
            (pl.BlockSpec((rows, width), lambda s, info: (0, 0)), left),
            (pl.BlockSpec((rows, half), lambda s, info: (0, info[0])), right),
            (pl.BlockSpec(sums.shape, lambda s, info: (0, 0)), sums),
        ],
        [(pl.BlockSpec(shape, lambda s, info: (0, 0)), sds(shape, BRAIN))],
        flops=2 * rows * width * half, nbytes=4 * rows * (width + half), deps=deps, prefetch=1,
    )[0]


def space_outer(slot, *operands, deps=()):
    rows, width = operands[0].shape
    half = width * 5 // 2
    return call(
        space_outer_kernel, (1,),
        [(smem(), slot)] + [(whole(v.shape), v) for v in operands],
        [(whole((width, half)), sds((width, half), BRAIN))],
        flops=2 * rows * width * half, nbytes=4 * rows * (width + half), deps=deps,
    )[0]


def mlp_outer(slot, low, before, hidden, feed, deps=()):
    rows, width = low.shape
    wide = hidden.shape[1]
    shape = (BLOCKS, 4 * (width // BLOCKS), width)
    fixed = pl.BlockSpec((rows, width), lambda s, info: (0, 0))
    moving = pl.BlockSpec((rows, width), lambda s, info: (0, s))
    return call(
        mlp_outer_kernel, (wide // width,),
        [(None, slot), (fixed, low), (moving, before), (moving, hidden), (fixed, feed)],
        [(pl.BlockSpec(shape, lambda s, info: (0, 0, 0)), sds(shape, BRAIN))] * 2,
        flops=4 * rows * width * wide, nbytes=4 * rows * (wide + width), deps=deps, prefetch=1,
    )


def gate(value, deps):
    return pl.pallas_call(
        lambda source, *refs: None,
        in_specs=[hbm()] * (1 + len(deps)),
        out_specs=hbm(),
        out_shape=sds(value.shape, value.dtype),
        input_output_aliases={0: 0},
    )(value, *deps)


def stack_kernel(*refs):
    for n, ref in enumerate(refs[:-1]):
        refs[-1][n] = ref[...]


def add_kernel(left, right, out):
    out[...] = left[...] + right[...]


def add_after(left, right, deps):
    inputs = [(whole(left.shape), left), (whole(right.shape), right)]
    return call(add_kernel, (1,), inputs, [(whole(left.shape), sds(left.shape, left.dtype))], deps=deps)[0]


def assemble_kernel(info, o4, rx, ry, ra, rb, out):
    depth = info[2]
    plane = info[3]
    for m in range(4):
        for n in range(4):
            if n < 3:
                value = (o4, rx, ry)[n][m]
            else:
                value = ra[m] if m < 2 else rb[m - 2]
            out[(depth ^ m) * 4 + (plane ^ n)] = value


def pack_kernel(info, time_qkv, space_qkv, space_proj, time_proj, up, time_vec, space_vec, mlp_vec, bias, send, keep):
    width = time_proj.shape[1]
    half = width // 2
    pieces = [time_qkv[:, n * half : (n + 1) * half] for n in range(6)]
    pieces += [space_qkv[:, n * half : (n + 1) * half] for n in range(6)]
    pieces += [space_proj[:, :half], space_proj[:, half:], time_proj[:, :half], time_proj[:, half:]]
    pieces += [up[:, n * half : (n + 1) * half] for n in range(8)]
    first = info[0] == 0
    at = 0
    for begin, count in ((0, 3), (6, 5), (16, 4)):
        for n in range(count):
            low, high = pieces[begin + n], pieces[begin + count + n]
            keep[:, at : at + half] = jnp.where(first, low, high)
            send[:, at : at + half] = jnp.where(first, high, low)
            at += half
    line = 0
    total = jnp.zeros((keep.shape[0], LANES), FLOAT)
    for source in (time_vec, space_vec, mlp_vec, bias):
        count = source.shape[0]
        lane = lax.broadcasted_iota(jnp.int32, (count, LANES), 1)
        chosen = (lane == row_index((count, LANES)) + line).astype(FLOAT)
        total = total + lax.dot_general(
            source[...].astype(FLOAT), chosen, (((0,), (0,)), ((), ())), preferred_element_type=FLOAT
        )
        line += count
    keep[:, at:] = total.astype(BRAIN)
    send[:, at:] = total.astype(BRAIN)


def turn_kernel(source, out):
    out[...] = source[...].astype(FLOAT).T


def join_kernel(info, keep, come, down, time_out, space_out, mlp_out):
    first = info[0] == 0
    width = down.shape[1]
    mine, far = keep[...].astype(FLOAT), come[...].astype(FLOAT)
    both = jnp.concatenate([jnp.where(first, mine, far), jnp.where(first, far, mine)], axis=0).astype(BRAIN)
    cut = both.shape[0]
    end = time_out.shape[1] - LANES
    time_out[:, :end] = both[:, :end]
    time_out[:, end:] = both[:, both.shape[1] - LANES :]
    space_out[...] = both[:, end : end + space_out.shape[1]]
    at = end + space_out.shape[1]
    mlp_out[:cut] = both[:, at : at + width]
    mlp_out[cut : 2 * cut] = both[:, at + width : at + 2 * width]
    mlp_out[2 * cut :] = down[...]


def added(*values):
    return sum(v.astype(FLOAT) for v in values).astype(BRAIN)


def reduce_first_kernel(info, mine, far, to_y, to_x, near_x, near_y, own):
    step = pl.program_id(0)
    plane = info[3]
    own[0] = added(mine[0, plane], far[0, plane])
    near_x[0] = added(mine[0, plane ^ 1], far[0, plane ^ 1])
    near_y[0] = added(mine[0, plane ^ 2], far[0, plane ^ 2])
    diagonal = added(mine[0, plane ^ 3], far[0, plane ^ 3])

    @pl.when(step < 2)
    def _():
        to_y[0] = diagonal

    @pl.when(step >= 2)
    def _():
        to_x[0] = diagonal


def reduce_second_kernel(near_x, near_y, from_y, from_x, out_x, out_y):
    step = pl.program_id(0)

    @pl.when(step < 2)
    def _():
        out_x[0] = added(near_x[0], from_y[0])
        out_y[0] = near_y[0]

    @pl.when(step >= 2)
    def _():
        out_x[0] = near_x[0]
        out_y[0] = added(near_y[0], from_x[0])


def reduce_third_kernel(info, own, from_x, from_y, first, second, others):
    for m in range(4):
        at = info[2] ^ m
        value = added(own[at], from_x[at], from_y[at])
        if m == 0:
            first[...] = value
        elif m == 1:
            second[...] = value
        else:
            others[m - 2] = value


def reduce_fourth_kernel(first, second, come, first_out, second_out):
    first_out[...] = first[...].astype(FLOAT) + come[0].astype(FLOAT)
    second_out[...] = added(second[...], come[1])


def clip_swap(values, bits, count):
    return lax.ppermute(values, "clip", [(i, i ^ bits) for i in range(count)])


def core_swap(values):
    return lax.ppermute(values, "frame", [(0, 1), (1, 0)])


class Near:
    def __init__(self, clips, info):
        self.clips = clips
        self.info = info
        self.core = lax.axis_index("frame")

    def swap(self, values, bits):
        return clip_swap(values, bits, self.clips)

    def in_order(self, mine, far, axis):
        return jnp.where(
            self.core == 0, jnp.concatenate([mine, far], axis=axis), jnp.concatenate([far, mine], axis=axis)
        )

    def stack(self, pieces, deps):
        shape = (len(pieces),) + pieces[0].shape
        return call(
            stack_kernel, (1,), [(whole(v.shape), v) for v in pieces], [(whole(shape), sds(shape, BRAIN))],
            nbytes=4 * len(pieces) * pieces[0].size, deps=deps,
        )[0]

    def depth_direct(self, own, deps):
        return self.stack([own] + [self.swap(own, 4 * m) for m in (1, 2, 3)], deps)

    def depth_near(self, own, deps):
        return self.stack([own, self.swap(own, 4)], deps)

    def depth_far(self, two, deps):
        come = self.swap(two, 8)
        return self.stack([two[0], two[1], come[0], come[1]], deps)

    def plane_step(self, o4, deps):
        rx = self.swap(o4, 1)
        ry = self.swap(o4, 2)
        if deps:
            rx, ry = gate(rx, deps), gate(ry, deps)
        return rx, ry, rx[:2], ry[2:]

    def diagonal_step(self, o4, planes, deps):
        rx, ry, sx, sy = planes
        pieces = (o4, rx, ry, self.swap(sx, 2), self.swap(sy, 1))
        shape = (self.clips,) + o4.shape[1:]
        return call(
            assemble_kernel, (1,), [(smem(), self.info)] + [(whole(v.shape), v) for v in pieces],
            [(whole(shape), sds(shape, BRAIN))], nbytes=16 * o4.size, deps=deps,
        )[0]

    def reduce_first(self, mine, far, deps):
        block = mine.shape[1:]
        four = (4, 4) + block
        view = pl.BlockSpec((1, 4) + block, lambda s: (s, 0, 0, 0))
        one = lambda pick: pl.BlockSpec((1,) + block, lambda s: (pick(s), 0, 0))
        each = (one(lambda s: s), sds((4,) + block, BRAIN))
        return call(
            reduce_first_kernel, (4,),
            [(smem(), self.info), (view, mine.reshape(four)), (view, far.reshape(four))],
            [
                (one(lambda s: jnp.minimum(s, 1)), sds((2,) + block, BRAIN)),
                (one(lambda s: jnp.maximum(s - 2, 0)), sds((2,) + block, BRAIN)),
                each, each, each,
            ],
            nbytes=6 * mine.size, deps=deps,
        )

    def reduce_second(self, near_x, near_y, to_y, to_x, deps):
        from_y, from_x = self.swap(to_y, 2), self.swap(to_x, 1)
        block = near_x.shape[1:]
        one = lambda pick: pl.BlockSpec((1,) + block, lambda s: (pick(s), 0, 0))
        each = one(lambda s: s)
        return call(
            reduce_second_kernel, (4,),
            [
                (each, near_x), (each, near_y), (one(lambda s: jnp.minimum(s, 1)), from_y),
                (one(lambda s: jnp.maximum(s - 2, 0)), from_x),
            ],
            [(each, sds(near_x.shape, BRAIN))] * 2, nbytes=10 * near_x.size, deps=deps,
        )

    def reduce_third(self, own, near_x, near_y, deps):
        from_x, from_y = self.swap(near_x, 1), self.swap(near_y, 2)
        block = own.shape[1:]
        return call(
            reduce_third_kernel, (1,),
            [(smem(), self.info)] + [(whole(v.shape), v) for v in (own, from_x, from_y)],
            [(whole(shape), sds(shape, BRAIN)) for shape in (block, block, (2,) + block)],
            nbytes=8 * own.size, deps=deps,
        )

    def reduce_fourth(self, first, second, others, deps):
        come = self.swap(others, 8)
        inputs = [(whole(v.shape), v) for v in (first, second, come)]
        outs = [(whole(first.shape), sds(first.shape, kind)) for kind in (FLOAT, BRAIN)]
        return call(reduce_fourth_kernel, (1,), inputs, outs, nbytes=8 * first.size, deps=deps)

    def reduce_end(self, first, second):
        return first + self.swap(second, 4).astype(FLOAT)

    def reduce_direct(self, first, second, others):
        total = first.astype(FLOAT) + self.swap(second, 4).astype(FLOAT)
        return total + self.swap(others[0], 8).astype(FLOAT) + self.swap(others[1], 12).astype(FLOAT)

    def owner_rows(self, value):
        rows = value.shape[0] // 2
        mine = lax.dynamic_slice_in_dim(value, self.core * rows, rows, 0)
        theirs = lax.dynamic_slice_in_dim(value, (1 - self.core) * rows, rows, 0)
        return self.in_order(mine, core_swap(theirs), 1)


AXES = ("clip", "frame")


def body(
    clips, cores, clip_tokens, clip_class, output_grad, class_grad, clip_count,
    time_qkv, time_proj, time_vec, space_qkv, space_proj, space_vec, mlp_up, mlp_down, mlp_vec, mlp_bias,
):
    _, own, places_here, width = clip_tokens.shape
    rows = -(-(places_here + 1) // 16) * 16
    frames = own * cores
    wide = mlp_up.shape[1]
    cut = width // BLOCKS
    core = lax.axis_index("frame")
    place = lax.axis_index("clip")
    shard = place * cores + core
    leader = (core == 0).astype(jnp.int32)
    alive = (jnp.arange(1, dtype=jnp.int32) < clip_count[0]).astype(FLOAT)
    is_near = clips == 16 and cores == 2
    slot = core if is_near else core * 0
    info = jnp.stack([slot, leader, place // 4, place % 4, shard]).astype(jnp.int32)
    near = Near(clips, info) if is_near else None
    my_slot = info[0:1]
    far_slot = 1 - my_slot

    class_block = jnp.broadcast_to(clip_class[0][None, None], (own, 1, width))
    blank = jnp.zeros((own, rows - places_here - 1, width), BRAIN)
    tokens = jnp.concatenate([clip_tokens[0], class_block, blank], axis=1)
    last = (jnp.arange(own) == own - 1)[:, None, None]
    class_rows = jnp.where(last, class_grad[0][None, None], jnp.zeros((), BRAIN))
    grads = jnp.concatenate([output_grad[0], class_rows, blank], axis=1)

    bias_rows = wide // width
    zeros = jnp.zeros((8, width), FLOAT)
    flat = lambda v: v.reshape((own * rows,) + v.shape[2:])

    if near is not None:
        packed = (
            time_qkv, space_qkv, space_proj, time_proj, mlp_up, time_vec, space_vec, mlp_vec,
            mlp_bias.reshape(-1, bias_rows).T,
        )
        line = sds((time_qkv.shape[0], 6 * width + LANES), BRAIN)
        send, keep = call(
            pack_kernel, (1,), [(smem(), info)] + [(whole(v.shape), v) for v in packed],
            [(whole(line.shape), line), (whole(line.shape), line)],
        )
        shapes = [(cut, 3 * width // 2 + LANES), (cut, 5 * width // 2), (4 * cut, width)]
        time_own, space_own, mlp_own = call(
            join_kernel, (1,),
            [(smem(), info)] + [(whole(v.shape), v) for v in (keep, core_swap(send), mlp_down)],
            [(whole(shape), sds(shape, BRAIN)) for shape in shapes],
        )
        join = lambda two: tuple(h.reshape(width, h.shape[-1]) for h in two)
        time_line = near.depth_direct(time_own, [])
        all_tokens = jnp.concatenate([tokens, core_swap(gate(tokens, [time_own]))], axis=0)
        space_own = gate(space_own, [time_line])
        space_line = near.depth_direct(space_own, [])
        time_mine = near.diagonal_step(time_line, near.plane_step(time_line, []), [grads, all_tokens, space_line])
        space_line = gate(space_line, [time_mine])
        time_far = core_swap(time_mine)
        time_w = join((time_mine, time_far))
        vec_block = pl.BlockSpec((width, LANES), lambda s: (0, time_w[0].shape[1] // LANES - 1))
        vectors = call(
            turn_kernel, (1,), [(vec_block, time_w[0])], [(whole((LANES, width)), sds((LANES, width), FLOAT))],
            deps=[space_line],
        )[0]
        n_vec = time_vec.shape[0] + space_vec.shape[0] + mlp_vec.shape[0]
        bias = vectors[n_vec : n_vec + bias_rows].T.reshape(bias_rows, width)
        mlp_own = gate(mlp_own, [time_far, space_line])
        mix_deps = [space_line, mlp_own]
    else:
        everywhere = lax.all_gather(tokens, "frame", axis=0, tiled=True)
        all_tokens = jnp.roll(everywhere, -core * own, axis=0)
        vec_shard = jnp.concatenate([time_vec, space_vec, mlp_vec], axis=0)
        blank_rows = jnp.zeros((16 - vec_shard.shape[0], width), FLOAT)
        space_shard = jnp.concatenate([space_qkv, space_proj, time_proj], axis=1)
        vectors = lax.all_gather(vec_shard, AXES, axis=1, tiled=True).astype(FLOAT)
        bias = lax.all_gather(mlp_bias, AXES, axis=0, tiled=True).astype(FLOAT).reshape(bias_rows, width)
        vectors = jnp.concatenate([vectors, blank_rows], axis=0)

        def halves(value):
            full = lax.all_gather(value, AXES, axis=0, tiled=True)
            half = full.shape[1] // 2
            return full[:, :half], full[:, half:]

        time_w, space_w = halves(time_qkv), halves(space_shard)
        up = lax.all_gather(mlp_up, AXES, axis=0, tiled=True).reshape(BLOCKS, cut, 2, 2, width)
        up = jnp.transpose(up, (2, 0, 3, 1, 4)).reshape(2, BLOCKS, 2 * cut, width)
        down = lax.all_gather(mlp_down, AXES, axis=0, tiled=True).reshape(BLOCKS, 2, 2 * cut, width)
        mlp_w = tuple(jnp.concatenate([up[n], down[:, n]], axis=1) for n in (0, 1))
        mix_deps = []

    frame_shape = (own, rows, width)
    all_shape = (frames, rows, width)
    heads = width // HEAD_DIM
    prob_shape = (own, frames, rows, LANES)
    sprob_shape = (own, heads, rows, rows)
    mixed_shape = (own, rows, 3 * width)
    hidden_shape = (own, rows, wide)
    sum_out = (whole((8, width)), sds((8, width), FLOAT))
    row_bytes = own * rows * width
    square = 2 * own * rows * width * width
    low_out = lambda shape, first=0: (per_frame(shape, first), sds(shape, BRAIN))
    wide_out = lambda shape, first=0: (per_frame(shape, first), sds(shape, FLOAT))
    vec_in = (whole(vectors.shape), vectors)
    pair = lambda two: [(hbm(), two[0]), (hbm(), two[1])]
    time_held = [pltpu.VMEM((width, 3 * width), BRAIN), pltpu.SemaphoreType.DMA((2,))]
    space_held = [pltpu.VMEM((width, 5 * width), BRAIN), pltpu.SemaphoreType.DMA((2,))]
    mlp_held = [
        pltpu.VMEM((wide // width, BLOCKS, cut, width), BRAIN),
        pltpu.VMEM((BLOCKS, 2, 2 * cut, width), BRAIN),
        pltpu.SemaphoreType.DMA((6,)),
    ]

    own_map = pl.BlockSpec((1, rows, width), lambda s: (jnp.minimum(s, own - 1), 0, 0))
    queries, key_rows, value_rows, time_low = call(
        functools.partial(time_mix_kernel, own), (frames,),
        [(smem(), info), (per_frame(all_shape), all_tokens), vec_in] + pair(time_w),
        [(own_map, sds(frame_shape, BRAIN)), low_out(all_shape), low_out(all_shape), (own_map, sds(frame_shape, BRAIN))],
        time_held, flops=5 * square, nbytes=20 * row_bytes, deps=mix_deps,
    )

    if near is not None:
        mlp_line = near.depth_direct(mlp_own, [])
        space_mine = near.diagonal_step(space_line, near.plane_step(space_line, [queries, mlp_line]), [])
        space_w = join((space_mine, core_swap(space_mine)))
        mlp_line = gate(mlp_line, [space_mine])

    parts = [(0, own)] if near is None else [(0, own // 2), (own // 2, own - own // 2)]
    deps = [] if near is None else [mlp_line]
    kept, class_own = (), zeros
    for first, count in parts:
        outs = call(
            functools.partial(attention_kernel, places_here), (count,),
            [
                (smem(), info), (per_frame(frame_shape, first), tokens), vec_in, (per_frame(frame_shape, first), queries),
                (whole(all_shape), key_rows), (whole(all_shape), value_rows), (whole((8, width)), class_own),
            ]
            + pair(space_w),
            [
                low_out(prob_shape, first), low_out(frame_shape, first), wide_out(frame_shape, first),
                low_out(frame_shape, first), low_out(mixed_shape, first), low_out(sprob_shape, first),
                low_out(frame_shape, first), wide_out(frame_shape, first), sum_out,
            ],
            space_held, flops=15 * square * count // own, nbytes=40 * row_bytes * count // own,
            deps=deps, previous=kept,
        )
        kept, class_own = tuple(outs[:-1]), outs[-1]
        if near is not None and first == 0:
            mlp_planes = near.plane_step(mlp_line, [class_own])
            deps = list(mlp_planes[2:])
    time_prob, time_att, after, space_low, space_mixed, space_prob, space_att, places = kept

    if near is not None:
        mlp_mine = near.diagonal_step(mlp_line, mlp_planes, [places])
        mlp_w = (mlp_mine, core_swap(mlp_mine))
        class_far = core_swap(class_own)
    else:
        class_far = lax.psum(class_own, "frame") - class_own
    class_row = jnp.broadcast_to(clip_class.astype(FLOAT), (8, width))
    small = whole((8, width))
    result, mlp_low, hidden, feed_grad, before_grad, rows_grad, mlp_sums = call(
        functools.partial(mlp_kernel, places_here, frames), (own,),
        [
            (smem(), info), (smem(), alive), (per_frame(frame_shape), places), (per_frame(frame_shape), grads),
            (small, class_row), (small, class_own), (small, class_far), vec_in, (whole(bias.shape), bias),
        ]
        + pair(mlp_w),
        [
            low_out(frame_shape), low_out(frame_shape), low_out(hidden_shape), low_out(frame_shape),
            low_out(hidden_shape), wide_out(frame_shape), sum_out,
        ],
        [pltpu.VMEM((wide // width, rows, width), FLOAT)] + mlp_held,
        flops=30 * square, nbytes=40 * row_bytes,
    )

    mlp_mine, mlp_far = mlp_outer(my_slot, flat(mlp_low), flat(before_grad), flat(hidden), flat(feed_grad))
    class_block_at = places_here // 16
    class_spec = pl.BlockSpec((1, 16, width), lambda s: (own - 1, class_block_at, 0))

    def space_back(first, count, sums, deps, previous):
        return call(
            functools.partial(space_back_kernel, places_here, frames), (count,),
            [
                (smem(), info), (per_frame(frame_shape, first), rows_grad), (class_spec, rows_grad),
                (per_frame(frame_shape, first), after), (per_frame(mixed_shape, first), space_mixed),
                (per_frame(sprob_shape, first), space_prob), vec_in, (small, sums),
            ]
            + pair(space_w),
            [
                low_out(frame_shape, first), low_out(mixed_shape, first), wide_out(frame_shape, first),
                low_out(frame_shape, first), low_out(frame_shape, first), sum_out,
            ],
            space_held, flops=20 * square * count // own, nbytes=40 * row_bytes * count // own,
            deps=deps, previous=previous,
        )

    half = own // 2
    if near is not None:
        outs = space_back(0, half, zeros, [mlp_far], ())
        mlp_a, mlp_b, mlp_x, mlp_y, mlp_own = near.reduce_first(mlp_mine, core_swap(mlp_far), [outs[0]])
        outs = space_back(half, own - half, outs[-1], [mlp_a, mlp_b], tuple(outs[:-1]))
        mlp_x, mlp_y = near.reduce_second(mlp_x, mlp_y, mlp_a, mlp_b, [outs[0]])
        time_deps = [mlp_x, mlp_y]
    else:
        outs = space_back(0, own, zeros, [], ())
        time_deps = []
    branch_grad, space_mixed_grad, after_grad, time_grad, time_att_grad, space_sums = outs

    far_frames = frames - own
    q_grad, own_grad, far_grad = call(
        time_back_kernel, (1,),
        [(whole(v.shape), v) for v in (queries, key_rows, value_rows, time_prob, time_att_grad)],
        [
            (whole(shape), sds(shape, BRAIN))
            for shape in (frame_shape, (2,) + frame_shape, (2, far_frames, rows, width))
        ],
        flops=6 * square, nbytes=40 * row_bytes, deps=time_deps,
    )
    operands = [flat(v) for v in (space_low, space_mixed_grad, space_att, branch_grad, time_att, time_grad)]
    if near is not None:
        from_far = core_swap(far_grad)
        mlp_parts = near.reduce_third(mlp_own, mlp_x, mlp_y, [q_grad])
        mlp_first, mlp_second, mlp_others = mlp_parts
        space_far = space_outer(far_slot, *operands, deps=[far_grad, mlp_second])
        space_mine = space_outer(my_slot, *operands, deps=[space_far])
        blocked = lambda v: v.reshape(BLOCKS, cut, v.shape[1])
        space_a, space_b, space_x, space_y, space_own = near.reduce_first(
            blocked(space_mine), core_swap(blocked(space_far)), [from_far]
        )
    else:
        padded = jnp.concatenate([jnp.zeros_like(own_grad), far_grad], axis=1)
        padded = jnp.roll(padded, core * own, axis=1)
        from_far = lax.psum_scatter(padded, "frame", scatter_dimension=1, tiled=True)
        space_mine, space_far = space_outer(my_slot, *operands), space_outer(far_slot, *operands)
    both = (own_grad.astype(FLOAT) + from_far.astype(FLOAT)).astype(BRAIN)
    time_mixed_grad = jnp.concatenate([q_grad, both[0], both[1]], axis=-1)
    outer = (flat(time_low), flat(time_mixed_grad))

    back_deps = [] if near is None else [space_a, space_b]
    token_grad, time_sums = call(
        time_mix_back_kernel, (own,),
        [
            (smem(), info), (per_frame(frame_shape), tokens), vec_in, (per_frame(mixed_shape), time_mixed_grad),
            (per_frame(frame_shape), after_grad),
        ]
        + pair(time_w),
        [wide_out(frame_shape), sum_out],
        time_held, flops=3 * square, nbytes=30 * row_bytes, deps=back_deps,
    )
    bias_grad = mlp_sums[3 : 3 + bias_rows].reshape(width, bias_rows)
    sums = jnp.concatenate([time_sums[:4], space_sums[5:6], space_sums[:5], mlp_sums[:3]], axis=0).T
    n_sums = sums.shape[1]
    blank = jnp.zeros((width, LANES - n_sums - bias_rows), FLOAT)
    sums = jnp.concatenate([sums, bias_grad, blank], axis=1)

    if near is not None:
        mlp_grads = near.reduce_direct(mlp_first, mlp_second, mlp_others)
        space_x, space_y = near.reduce_second(space_x, space_y, space_a, space_b, [token_grad])
        time_far = time_outer(far_slot, *outer, sums, deps=[space_x, space_y])
        time_mine = time_outer(my_slot, *outer, sums, deps=[time_far])
        space_parts = near.reduce_third(space_own, space_x, space_y, [time_mine])
        time_a, time_b, time_x, time_y, time_own = near.reduce_first(
            blocked(time_mine), core_swap(blocked(time_far)), []
        )
        time_x, time_y = near.reduce_second(time_x, time_y, time_a, time_b, [space_parts[1]])
        time_parts = near.reduce_third(time_own, time_x, time_y, [])
        grad_space = near.owner_rows(near.reduce_direct(*space_parts))
        total = near.reduce_direct(*time_parts)
        half = 3 * width // 2
        grad_time = near.owner_rows(total[:, :half])
        step = cut // 2
        sums = lax.dynamic_slice_in_dim(total[:, half:], core * step, step, 0)
        grad_mlp_down = mlp_grads[2 * cut :]
        grad_mlp_up = near.owner_rows(jnp.concatenate([mlp_grads[:cut], mlp_grads[cut : 2 * cut]], axis=1))
        class_total = space_sums[6:7] + core_swap(space_sums)[6:7]
    else:
        send = lambda v: lax.psum_scatter(v, AXES, scatter_dimension=0, tiled=True).astype(FLOAT)
        time_mine, time_far = (time_outer(slot, *outer, sums)[:, : 3 * width // 2] for slot in (my_slot, far_slot))
        up = jnp.stack([v[:, : 2 * cut].reshape(BLOCKS, 2, cut, width) for v in (mlp_mine, mlp_far)])
        grad_mlp_up = send(jnp.transpose(up, (1, 3, 0, 2, 4)).reshape(width, wide))
        grad_mlp_down = send(jnp.stack([v[:, 2 * cut :] for v in (mlp_mine, mlp_far)], axis=1).reshape(wide, width))
        grad_space = send(jnp.concatenate([space_mine, space_far], axis=1))
        grad_time = send(jnp.concatenate([time_mine, time_far], axis=1))
        class_total = lax.psum(space_sums[6:7], "frame")
        step = width // (clips * cores)
        sums = lax.dynamic_slice_in_dim(lax.psum(sums, AXES), shard * step, step, 0)
    class_in_grad = rows_grad[own - 1, places_here][None] + class_total
    lines = sums.T
    grad_time_vec, grad_space_vec, grad_mlp_vec = lines[:5], lines[5:10], lines[10:13]
    grad_mlp_bias = sums[:, n_sums : n_sums + bias_rows].reshape(-1)
    return (
        result[:, :places_here][None],
        result[own - 1, places_here][None],
        token_grad[:, :places_here][None],
        class_in_grad,
        grad_time,
        grad_space[:, 4 * width :],
        grad_time_vec,
        grad_space[:, : 3 * width],
        grad_space[:, 3 * width : 4 * width],
        grad_space_vec,
        grad_mlp_up,
        grad_mlp_down,
        grad_mlp_vec,
        grad_mlp_bias,
    )


def solution(mesh):
    both = ("clip", "frame")
    rows = P(both, None)
    columns = P(None, both)
    weights = (rows, rows, columns, rows, rows, columns, rows, rows, columns, P(both))
    block = P("clip", "frame", None, None)
    classes = P("clip", None)
    return jax.shard_map(
        functools.partial(body, mesh.shape["clip"], mesh.shape["frame"]),
        mesh=mesh,
        in_specs=(block, classes, block, classes, P("clip")) + weights,
        out_specs=(block, classes, block, classes) + weights,
        check_vma=False,
    )
```

profile of v0, /device:TPU:0, one launch (start us, length us, event | category | flops | bytes accessed | tf_op | source)
XLA Modules:
  0.0 477.7 jit_solution(9981079944810398970)
XLA Ops:
  24.1 6.3 %collective-permute-done.2.refs_2_ = bf16[48,1280]{1,0:T(8,128)(2,1)S(1)} collective-permute-done((bf16[48,1280]{1,0:T(8,128)(2,1)S(1)}, bf16[48,1280]{1,0:T(8,128)(2,1)S(1)}, u32[]{:S(2)}, u32[]{:S(2)}) %collective-permute-start.2) | collective-permute-done | bytes 122912 | tf_op jit(solution)/shard_map/ppermute | solution.py:643
  75.9 14.0 %shard_map.267 = (bf16[4,208,768]{2,1,0:T(8,128)(2,1)}, bf16[8,208,768]{2,1,0:T(8,128)(2,1)}, bf16[8,208,768]{2,1,0:T(8,128)(2,1)}, bf16[4,208,768]{2,1,0:T(8,128)(2,1)}) custom-call(s32[5]{0:T(128)} %stack.27.refs_0_, bf16[8,208,768]{2,1,0:T(8,128)(2,1)} %pad_maximum_fusion.2.refs_7_.refs_1_, f32[128,768]{1,0:T(8,128)} %shard_map.265.refs_2_.refs_7_.refs_6_, ...), custom_call_target="tpu_custom_call" | custom-call | flops 1 | bytes 1 | tf_op jit(solution)/shard_map/pallas_call | solution.py:460
  89.9 4.7 collective-permute-done.15.refs_2_
  103.2 5.5 %collective-permute-done.19.refs_5_ = bf16[2,48,1920]{2,1,0:T(8,128)(2,1)S(1)} collective-permute-done((bf16[2,48,1920]{2,1,0:T(8,128)(2,1)S(1)}, bf16[2,48,1920]{2,1,0:T(8,128)(2,1)S(1)}, u32[]{:S(2)}, u32[]{:S(2)}) %collective-permute-start.19) | collective-permute-done | bytes 368672 | tf_op jit(solution)/shard_map/ppermute | solution.py:643
  122.2 17.7 %shard_map.273 = (bf16[4,8,208,128]{3,2,1,0:T(8,128)(2,1)}, bf16[4,208,768]{2,1,0:T(8,128)(2,1)}, f32[4,208,768]{2,1,0:T(8,128)}, bf16[4,208,768]{2,1,0:T(8,128)...) custom-call(s32[5]{0:T(128)} %stack.27.refs_0_, ...), custom_call_target="tpu_custom_call" | custom-call | flops 1 | bytes 1 | tf_op jit(solution)/shard_map/pallas_call | solution.py:460
  148.4 17.9 %shard_map.276 = (bf16[4,8,208,128]{3,2,1,0:T(8,128)(2,1)}, bf16[4,208,768]{2,1,0:T(8,128)(2,1)}, f32[4,208,768]{2,1,0:T(8,128)}, bf16[4,208,768]{2,1,0:T(8,128)...) custom-call(s32[5]{0:T(128)} %stack.27.refs_0_, ...), custom_call_target="tpu_custom_call", output_to_operand_aliasing={{0}: (9, {}), {1}: (10, {}), {2}: (11, {}), {3}: (12, {}), ... | custom-call | flops 1 | bytes 1 | tf_op jit(solution)/shard_map/pallas_call | solution.py:460
  167.3 4.8 %shard_map.277.refs_9_ = bf16[16,192,768]{2,1,0:T(8,128)(2,1)} custom-call(s32[5]{0:T(128)} %stack.27.refs_0_, bf16[4,192,768]{2,1,0:T(8,128)(2,1)} %shard_map.272.refs_9_.refs_1_, bf16[4,192,768]{2,1,0:T(8,128)(2,1)} %shard_map.274.refs_2_, bf16[4,192,768]{2,1,0:T(8,128)(2,1)} %shard_map.275.refs_3_, bf16[2,192,768]{2,1,0:T(8,128)(2,1)} %copy-done.27, ...), custom_call_target="tpu_custom_call" | custom-call | flops 1 | bytes 1 | tf_op jit(solution)/shard_map/pallas_call | solution.py:460
  175.2 4.9 %collective-permute-done.23.refs_6_ = f32[8,768]{1,0:T(8,128)S(1)} collective-permute-done((f32[8,768]{1,0:T(8,128)S(1)}, f32[8,768]{1,0:T(8,128)S(1)}, u32[]{:S(2)}, u32[]{:S(2)}) %collective-permute-start.23) | collective-permute-done | bytes 24608 | tf_op jit(solution)/shard_map/ppermute | solution.py:647
  181.0 28.1 %shard_map.278 = (bf16[4,208,768]{2,1,0:T(8,128)(2,1)}, bf16[4,208,768]{2,1,0:T(8,128)(2,1)}, bf16[4,208,3072]{2,1,0:T(8,128)(2,1)}, bf16[4,208,768]{2,1,0:T(8,1...) custom-call(s32[5]{0:T(128)} %stack.27.refs_0_, ...), custom_call_target="tpu_custom_call" | custom-call | flops 1 | bytes 1 | tf_op jit(solution)/shard_map/pallas_call | solution.py:460
  209.1 21.6 %shard_map.279 = (bf16[16,192,768]{2,1,0:T(8,128)(2,1)}, bf16[16,192,768]{2,1,0:T(8,128)(2,1)}) custom-call(s32[1]{0:T(128)} %bitcast.refs_0_, bf16[832,768]{1,0:T(8,128)(2,1)} %bitcast.111, bf16[832,3072]{1,0:T(8,128)(2,1)} %bitcast.101, bf16[832,3072]{1,0:T(8,128)(2,1)} %bitcast.100, bf16[832,768]{1,0:T(8,128)(2,1)} %bitcast.112), custom_call_target="tpu_custom_call" | custom-call | flops 1 | bytes 1 | tf_op jit(solution)/shard_map/pallas_call | solution.py:460
  230.8 19.6 %shard_map.280 = (bf16[4,208,768]{2,1,0:T(8,128)(2,1)}, bf16[4,208,2304]{2,1,0:T(8,128)(2,1)}, f32[4,208,768]{2,1,0:T(8,128)}, bf16[4,208,768]{2,1,0:T(8,128)(2,...) custom-call(s32[5]{0:T(128)} %stack.27.refs_0_, f32[4,208,768]{2,1,0:T(8,128)} %get-tuple-element.118.refs_1_.refs_2_, ...), custom_call_target="tpu_custom_call" | custom-call | flops 1 | bytes 1 | tf_op jit(solution)/shard_map/pallas_call | solution.py:460
  252.6 6.7 %shard_map.281 = (bf16[2,192,768]{2,1,0:T(8,128)(2,1)}, bf16[2,192,768]{2,1,0:T(8,128)(2,1)}, bf16[4,192,768]{2,1,0:T(8,128)(2,1)}, bf16[4,192,768]{2,1,0:T(8,128)(2,1)}, bf16[4,192,768]{2,1,0:T(8,128)(2,1)}) custom-call(s32[5]{0:T(128)} %stack.27.refs_0_, bf16[4,4,192,768]{3,2,1,0:T(8,128)(2,1)} %bitcast.107, bf16[4,4,192,768]{3,2,1,0:T(8,128)(2,1)} %bitcast.108, ...), custom_call_target="tpu_custom_call" | custom-call | flops 1 | bytes 1 | tf_op jit(solution)/shard_map/pallas_call | solution.py:460
  261.3 19.9 %shard_map.282 = (bf16[4,208,768]{2,1,0:T(8,128)(2,1)}, bf16[4,208,2304]{2,1,0:T(8,128)(2,1)}, f32[4,208,768]{2,1,0:T(8,128)}, bf16[4,208,768]{2,1,0:T(8,128)(2,...) custom-call(s32[5]{0:T(128)} %stack.27.refs_0_, ...), custom_call_target="tpu_custom_call", output_to_operand_aliasing={{0}: (10, {}), {1}: (11, {}), {2}: (12, {}), {3}: (13, {}),... | custom-call | flops 1 | bytes 1 | tf_op jit(solution)/shard_map/pallas_call | solution.py:460
  288.6 22.5 %shard_map.284 = (bf16[4,208,768]{2,1,0:T(8,128)(2,1)}, bf16[2,4,208,768]{3,2,1,0:T(8,128)(2,1)}, bf16[2,4,208,768]{3,2,1,0:T(8,128)(2,1)}) custom-call(bf16[4,208,768]{2,1,0:T(8,128)(2,1)} %get-tuple-element.102.refs_0_.refs_3_, bf16[8,208,768]{2,1,0:T(8,128)(2,1)} %get-tuple-element.103.refs_4_.refs_1_, ...), custom_call_target="tpu_custom_call" | custom-call | flops 1 | bytes 1 | tf_op jit(solution)/shard_map/pallas_call | solution.py:460
  320.2 9.2 %shard_map.286.refs_7_ = bf16[768,1920]{1,0:T(8,128)(2,1)} custom-call(s32[1]{0:T(128)S(6)} %sub.13.refs_0_, bf16[832,768]{1,0:T(8,128)(2,1)} %bitcast.90, bf16[832,2304]{1,0:T(8,128)(2,1)} %bitcast.79, bf16[832,768]{1,0:T(8,128)(2,1)} %bitcast.92, bf16[832,768]{1,0:T(8,128)(2,1)} %bitcast.81, bf16[832,768]{1,0:T(8,128)(2,1)} %bitcast.88, ...), custom_call_target="tpu_custom_call" | custom-call | flops 1 | bytes 1 | tf_op jit(solution)/shard_map/pallas_call | solution.py:460
  335.7 6.2 %collective-permute-start.52 = (bf16[192,768]{1,0:T(8,128)(2,1)}, bf16[192,768]{1,0:T(8,128)(2,1)S(1)}, u32[]{:S(2)}, u32[]{:S(2)}) collective-permute-start(bf16[192,768]{1,0:T(8,128)(2,1)} %get-tuple-element.152.refs_8_), channel_id=1, source_target_pairs={{0,8},{2,10},{4,12},{6,14},{8,0},{10,2},{12,4},{14,6},{16,24},{18,... | collective-permute-start | bytes 884744 | tf_op jit(solution)/shard_map/ppermute | solution.py:643
  341.9 8.9 %shard_map.287 = bf16[768,1920]{1,0:T(8,128)(2,1)} custom-call(s32[1]{0:T(128)} %bitcast.refs_0_, bf16[832,768]{1,0:T(8,128)(2,1)} %bitcast.91, bf16[832,2304]{1,0:T(8,128)(2,1)} %bitcast.80, bf16[832,768]{1,0:T(8,128)(2,1)} %bitcast.93, bf16[832,768]{1,0:T(8,128)(2,1)} %bitcast.82, bf16[832,768]{1,0:T(8,128)(2,1)} %bitcast.89, bf16[832,768]{1,0:T(8,128)(2,1)} %bitcast.95, ...), custom_call_target="tpu_custom_call" | custom-call | flops 1 | bytes 1 | tf_op jit(solution)/shard_map/pallas_call | solution.py:460
  361.5 5.2 %shard_map.288 = (bf16[2,48,1920]{2,1,0:T(8,128)(2,1)}, bf16[2,48,1920]{2,1,0:T(8,128)(2,1)}, bf16[4,48,1920]{2,1,0:T(8,128)(2,1)}, bf16[4,48,1920]{2,1,0:T(8,128)(2,1)}, bf16[4,48,1920]{2,1,0:T(8,128)(2,1)}) custom-call(s32[5]{0:T(128)} %stack.27.refs_0_, bf16[4,4,48,1920]{3,2,1,0:T(8,128)(2,1)} %bitcast.87, bf16[4,4,48,1920]{3,2,1,0:T(8,128)(2,1)} %bitcast.31.refs_2_, ...), custom_call_target="tpu_custom_call" | custom-call | flops 1 | bytes 1 | tf_op jit(solution)/shard_map/pallas_call | solution.py:460
  370.0 11.3 %shard_map.289 = (f32[4,208,768]{2,1,0:T(8,128)}, f32[8,768]{1,0:T(8,128)}) custom-call(s32[5]{0:T(128)} %stack.27.refs_0_, bf16[4,208,768]{2,1,0:T(8,128)(2,1)} %copy-done.1, f32[128,768]{1,0:T(8,128)} %shard_map.265.refs_2_.refs_7_.refs_6_, bf16[4,208,2304]{2,1,0:T(8,128)(2,1)} %pad_maximum_fusion.refs_3_, f32[4,208,768]{2,1,0:T(8,128)} %get-tuple-element.145.refs_4_, ...), custom_call_target="tpu_custom_call" | custom-call | flops 1 | bytes 1 | tf_op jit(solution)/shard_map/pallas_call | solution.py:460
  387.9 5.5 %shard_map.291.refs_4_ = bf16[768,1280]{1,0:T(8,128)(2,1)} custom-call(s32[1]{0:T(128)S(6)} %sub.13.refs_0_, bf16[832,768]{1,0:T(8,128)(2,1)} %bitcast.102, bf16[832,2304]{1,0:T(8,128)(2,1)} %pad_maximum_fusion.1.refs_2_, f32[768,128]{1,0:T(8,128)} %maximum_maximum_fusion.refs_3_, bf16[4,48,1920]{2,1,0:T(8,128)(2,1)} %get-tuple-element.162.refs_4_, ...), custom_call_target="tpu_custom_call" | custom-call | flops 1 | bytes 1 | tf_op jit(solution)/shard_map/pallas_call | solution.py:460
  400.5 5.5 %shard_map.292.refs_4_ = bf16[768,1280]{1,0:T(8,128)(2,1)} custom-call(s32[1]{0:T(128)} %bitcast.refs_0_, bf16[832,768]{1,0:T(8,128)(2,1)} %bitcast.103, bf16[832,2304]{1,0:T(8,128)(2,1)} %pad_maximum_fusion.1.refs_2_, f32[768,128]{1,0:T(8,128)} %maximum_maximum_fusion.refs_3_, bf16[768,1280]{1,0:T(8,128)(2,1)} %shard_map.291.refs_4_), custom_call_target="tpu_custom_call" | custom-call | flops 1 | bytes 1 | tf_op jit(solution)/shard_map/pallas_call | solution.py:460
  406.1 8.4 %collective-permute-done.40.refs_2_ = bf16[4,48,1920]{2,1,0:T(8,128)(2,1)S(1)} collective-permute-done((bf16[4,48,1920]{2,1,0:T(8,128)(2,1)S(1)}, bf16[4,48,1920]{2,1,0:T(8,128)(2,1)S(1)}, u32[]{:S(2)}, u32[]{:S(2)}) %collective-permute-start.40) | collective-permute-done | bytes 737312 | tf_op jit(solution)/shard_map/ppermute | solution.py:643
  447.2 7.8 %collective-permute-done.42.refs_2_ = bf16[4,48,1280]{2,1,0:T(8,128)(2,1)S(1)} collective-permute-done((bf16[4,48,1280]{2,1,0:T(8,128)(2,1)}, bf16[4,48,1280]{2,1,0:T(8,128)(2,1)S(1)}, u32[]{:S(2)}, u32[]{:S(2)}) %collective-permute-start.42) | collective-permute-done | bytes 491552 | tf_op jit(solution)/shard_map/ppermute | solution.py:643
  465.6 6.6 %collective-permute-done.45 = bf16[48,1280]{1,0:T(8,128)(2,1)S(1)} collective-permute-done((bf16[48,1280]{1,0:T(8,128)(2,1)S(1)}, bf16[48,1280]{1,0:T(8,128)(2,1)S(1)}, u32[]{:S(2)}, u32[]{:S(2)}) %collective-permute-start.45) | collective-permute-done | bytes 122912 | tf_op jit(solution)/shard_map/ppermute | solution.py:643
  (314 shorter events, 206.5 us)
Async XLA Ops:
  14.6 43.4 %collective-permute-start.8 = (bf16[4,208,768]{2,1,0:T(8,128)(2,1)}, bf16[4,208,768]{2,1,0:T(8,128)(2,1)S(1)}, u32[]{:S(2)}, u32[]{:S(2)}) collective-permute-start(bf16[4,208,768]{2,1,0:T(8,128)(2,1)} %shard_map.260), channel_id=1, source_target_pairs={{0,1},{1,0},{2,3},{3,2},{4,5},{5,4},{6,7},{7,6},{8,9},{9,8},{10,11... | collective-permute-start | bytes 3833864 | tf_op jit(solution)/shard_map/ppermute | solution.py:647
  64.2 34.1 %collective-permute-start.17 = (bf16[4,48,1920]{2,1,0:T(8,128)(2,1)}, bf16[4,48,1920]{2,1,0:T(8,128)(2,1)S(1)}, u32[]{:S(2)}, u32[]{:S(2)}) collective-permute-start(bf16[4,48,1920]{2,1,0:T(8,128)(2,1)} %shard_map.264.refs_1_.refs_5_), channel_id=1, source_target_pairs={{0,4},{2,6},{4,0},{6,2},{8,12},{10,14},{12,8},{14,10},{16,20},{18,... | collective-permute-start | bytes 2211848 | tf_op jit(solution)/shard_map/ppermute | solution.py:643
  64.7 36.1 %collective-permute-start.13 = (bf16[4,48,1920]{2,1,0:T(8,128)(2,1)}, bf16[4,48,1920]{2,1,0:T(8,128)(2,1)S(1)}, u32[]{:S(2)}, u32[]{:S(2)}) collective-permute-start(bf16[4,48,1920]{2,1,0:T(8,128)(2,1)} %shard_map.264.refs_1_.refs_5_), channel_id=1, source_target_pairs={{0,2},{2,0},{4,6},{6,4},{8,10},{10,8},{12,14},{14,12},{16,18},{18,... | collective-permute-start | bytes 2211848 | tf_op jit(solution)/shard_map/ppermute | solution.py:643
  69.7 20.2 %collective-permute-start.14 = (bf16[192,768]{1,0:T(8,128)(2,1)}, bf16[192,768]{1,0:T(8,128)(2,1)S(1)}, u32[]{:S(2)}, u32[]{:S(2)}) collective-permute-start(bf16[192,768]{1,0:T(8,128)(2,1)} %shard_map.266.refs_6_.refs_0_), channel_id=1, source_target_pairs={{0,8},{2,10},{4,12},{6,14},{8,0},{10,2},{12,4},{14,6},{16,24},{18,... | collective-permute-start | bytes 884744 | tf_op jit(solution)/shard_map/ppermute | solution.py:643
  70.9 23.6 %collective-permute-start.15 = (bf16[192,768]{1,0:T(8,128)(2,1)}, bf16[192,768]{1,0:T(8,128)(2,1)S(1)}, u32[]{:S(2)}, u32[]{:S(2)}) collective-permute-start(bf16[192,768]{1,0:T(8,128)(2,1)} %shard_map.266.refs_6_.refs_0_), channel_id=1, source_target_pairs={{0,16},{2,18},{4,20},{6,22},{8,24},{10,26},{12,28},{14,30},{16,0},... | collective-permute-start | bytes 884744 | tf_op jit(solution)/shard_map/ppermute | solution.py:643
  71.9 22.7 %collective-permute-start.16 = (bf16[192,768]{1,0:T(8,128)(2,1)}, bf16[192,768]{1,0:T(8,128)(2,1)S(1)}, u32[]{:S(2)}, u32[]{:S(2)}) collective-permute-start(bf16[192,768]{1,0:T(8,128)(2,1)} %shard_map.266.refs_6_.refs_0_), channel_id=1, source_target_pairs={{0,24},{2,26},{4,28},{6,30},{8,16},{10,18},{12,20},{14,22},{16,8},... | collective-permute-start | bytes 884744 | tf_op jit(solution)/shard_map/ppermute | solution.py:643
  115.0 28.7 %collective-permute-start.22 = (bf16[4,192,768]{2,1,0:T(8,128)(2,1)}, bf16[4,192,768]{2,1,0:T(8,128)(2,1)}, u32[]{:S(2)}, u32[]{:S(2)}) collective-permute-start(bf16[4,192,768]{2,1,0:T(8,128)(2,1)} %shard_map.272.refs_9_.refs_1_), channel_id=1, source_target_pairs={{0,4},{2,6},{4,0},{6,2},{8,12},{10,14},{12,8},{14,10},{16,20},{18,... | collective-permute-start | bytes 3538952 | tf_op jit(solution)/shard_map/ppermute | solution.py:643
  115.3 29.5 %collective-permute-start.21 = (bf16[4,192,768]{2,1,0:T(8,128)(2,1)}, bf16[4,192,768]{2,1,0:T(8,128)(2,1)}, u32[]{:S(2)}, u32[]{:S(2)}) collective-permute-start(bf16[4,192,768]{2,1,0:T(8,128)(2,1)} %shard_map.272.refs_9_.refs_1_), channel_id=1, source_target_pairs={{0,2},{2,0},{4,6},{6,4},{8,10},{10,8},{12,14},{14,12},{16,18},{18,... | collective-permute-start | bytes 3538952 | tf_op jit(solution)/shard_map/ppermute | solution.py:643
  146.2 20.1 %collective-permute-start.25 = (bf16[2,192,768]{2,1,0:T(8,128)(2,1)S(1)}, bf16[2,192,768]{2,1,0:T(8,128)(2,1)S(1)}, u32[]{:S(2)}, u32[]{:S(2)}) collective-permute-start(bf16[2,192,768]{2,1,0:T(8,128)(2,1)S(1)} %slice.157.refs_18_), channel_id=1, source_target_pairs={{0,2},{2,0},{4,6},{6,4},{8,10},{10,8},{12,14},{14,12},{16,18},{18,... | collective-permute-start | bytes 1769480 | tf_op jit(solution)/shard_map/ppermute | solution.py:643
  147.9 18.4 %collective-permute-start.24 = (bf16[2,192,768]{2,1,0:T(8,128)(2,1)S(1)}, bf16[2,192,768]{2,1,0:T(8,128)(2,1)S(1)}, u32[]{:S(2)}, u32[]{:S(2)}) collective-permute-start(bf16[2,192,768]{2,1,0:T(8,128)(2,1)S(1)} %slice.156.refs_17_), channel_id=1, source_target_pairs={{0,4},{2,6},{4,0},{6,2},{8,12},{10,14},{12,8},{14,10},{16,20},{18,... | collective-permute-start | bytes 1769480 | tf_op jit(solution)/shard_map/ppermute | solution.py:643
  230.7 19.7 %collective-permute-start.27 = (bf16[16,192,768]{2,1,0:T(8,128)(2,1)}, bf16[16,192,768]{2,1,0:T(8,128)(2,1)S(1)}, u32[]{:S(2)}, u32[]{:S(2)}) collective-permute-start(bf16[16,192,768]{2,1,0:T(8,128)(2,1)} %get-tuple-element.126.refs_10_), channel_id=1, source_target_pairs={{0,1},{1,0},{2,3},{3,2},{4,5},{5,4},{6,7},{7,6},{8,9},{9,8},{10,11... | collective-permute-start | bytes 14155784 | tf_op jit(solution)/shard_map/ppermute | solution.py:647
  259.3 21.9 %collective-permute-start.28 = (bf16[2,192,768]{2,1,0:T(8,128)(2,1)}, bf16[2,192,768]{2,1,0:T(8,128)(2,1)S(1)}, u32[]{:S(2)}, u32[]{:S(2)}) collective-permute-start(bf16[2,192,768]{2,1,0:T(8,128)(2,1)} %get-tuple-element.134.refs_15_), channel_id=1, source_target_pairs={{0,4},{2,6},{4,0},{6,2},{8,12},{10,14},{12,8},{14,10},{16,20},{18,... | collective-permute-start | bytes 1769480 | tf_op jit(solution)/shard_map/ppermute | solution.py:643
  261.0 20.2 %collective-permute-start.29 = (bf16[2,192,768]{2,1,0:T(8,128)(2,1)}, bf16[2,192,768]{2,1,0:T(8,128)(2,1)S(1)}, u32[]{:S(2)}, u32[]{:S(2)}) collective-permute-start(bf16[2,192,768]{2,1,0:T(8,128)(2,1)} %get-tuple-element.135.refs_16_), channel_id=1, source_target_pairs={{0,2},{2,0},{4,6},{6,4},{8,10},{10,8},{12,14},{14,12},{16,18},{18,... | collective-permute-start | bytes 1769480 | tf_op jit(solution)/shard_map/ppermute | solution.py:643
  286.5 27.9 %collective-permute-start.31 = (bf16[4,192,768]{2,1,0:T(8,128)(2,1)}, bf16[4,192,768]{2,1,0:T(8,128)(2,1)S(1)}, u32[]{:S(2)}, u32[]{:S(2)}) collective-permute-start(bf16[4,192,768]{2,1,0:T(8,128)(2,1)} %get-tuple-element.140.refs_5_), channel_id=1, source_target_pairs={{0,2},{2,0},{4,6},{6,4},{8,10},{10,8},{12,14},{14,12},{16,18},{18,... | collective-permute-start | bytes 3538952 | tf_op jit(solution)/shard_map/ppermute | solution.py:643
  288.2 27.6 %collective-permute-start.32 = (bf16[4,192,768]{2,1,0:T(8,128)(2,1)}, bf16[4,192,768]{2,1,0:T(8,128)(2,1)S(1)}, u32[]{:S(2)}, u32[]{:S(2)}) collective-permute-start(bf16[4,192,768]{2,1,0:T(8,128)(2,1)} %get-tuple-element.141.refs_6_), channel_id=1, source_target_pairs={{0,4},{2,6},{4,0},{6,2},{8,12},{10,14},{12,8},{14,10},{16,20},{18,... | collective-permute-start | bytes 3538952 | tf_op jit(solution)/shard_map/ppermute | solution.py:643
  311.1 43.1 %collective-permute-start.30 = (bf16[2,4,208,768]{3,2,1,0:T(8,128)(2,1)}, bf16[2,4,208,768]{3,2,1,0:T(8,128)(2,1)S(1)}, u32[]{:S(2)}, u32[]{:S(2)}) collective-permute-start(bf16[2,4,208,768]{3,2,1,0:T(8,128)(2,1)} %get-tuple-element.144.refs_7_), channel_id=1, source_target_pairs={{0,1},{1,0},{2,3},{3,2},{4,5},{5,4},{6,7},{7,6},{8,9},{9,8},{10,11... | collective-permute-start | bytes 7667720 | tf_op jit(solution)/shard_map/ppermute | solution.py:647
  329.4 32.2 %collective-permute-start.33 = (bf16[16,48,1920]{2,1,0:T(8,128)(2,1)}, bf16[16,48,1920]{2,1,0:T(8,128)(2,1)}, u32[]{:S(2)}, u32[]{:S(2)}) collective-permute-start(bf16[16,48,1920]{2,1,0:T(8,128)(2,1)} %bitcast.86), channel_id=1, source_target_pairs={{0,1},{1,0},{2,3},{3,2},{4,5},{5,4},{6,7},{7,6},{8,9},{9,8},{10,11... | collective-permute-start | bytes 8847368 | tf_op jit(solution)/shard_map/ppermute | solution.py:647
  335.7 62.8 %collective-permute-start.52 = (bf16[192,768]{1,0:T(8,128)(2,1)}, bf16[192,768]{1,0:T(8,128)(2,1)S(1)}, u32[]{:S(2)}, u32[]{:S(2)}) collective-permute-start(bf16[192,768]{1,0:T(8,128)(2,1)} %get-tuple-element.152.refs_8_), channel_id=1, source_target_pairs={{0,8},{2,10},{4,12},{6,14},{8,0},{10,2},{12,4},{14,6},{16,24},{18,... | collective-permute-start | bytes 884744 | tf_op jit(solution)/shard_map/ppermute | solution.py:643
  351.8 45.2 %collective-permute-start.53 = (bf16[192,768]{1,0:T(8,128)(2,1)}, bf16[192,768]{1,0:T(8,128)(2,1)S(1)}, u32[]{:S(2)}, u32[]{:S(2)}) collective-permute-start(bf16[192,768]{1,0:T(8,128)(2,1)} %get-tuple-element.228), channel_id=1, source_target_pairs={{0,16},{2,18},{4,20},{6,22},{8,24},{10,26},{12,28},{14,30},{16,0},... | collective-permute-start | bytes 884744 | tf_op jit(solution)/shard_map/ppermute | solution.py:643
  351.9 46.7 %collective-permute-start.54 = (bf16[192,768]{1,0:T(8,128)(2,1)}, bf16[192,768]{1,0:T(8,128)(2,1)}, u32[]{:S(2)}, u32[]{:S(2)}) collective-permute-start(bf16[192,768]{1,0:T(8,128)(2,1)} %get-tuple-element.229), channel_id=1, source_target_pairs={{0,24},{2,26},{4,28},{6,30},{8,16},{10,18},{12,20},{14,22},{16,8},... | collective-permute-start | bytes 884744 | tf_op jit(solution)/shard_map/ppermute | solution.py:643
  393.4 31.0 %collective-permute-start.37 = (bf16[16,48,1280]{2,1,0:T(8,128)(2,1)}, bf16[16,48,1280]{2,1,0:T(8,128)(2,1)S(1)}, u32[]{:S(2)}, u32[]{:S(2)}) collective-permute-start(bf16[16,48,1280]{2,1,0:T(8,128)(2,1)} %bitcast.99), channel_id=1, source_target_pairs={{0,1},{1,0},{2,3},{3,2},{4,5},{5,4},{6,7},{7,6},{8,9},{9,8},{10,11... | collective-permute-start | bytes 5898248 | tf_op jit(solution)/shard_map/ppermute | solution.py:647
  395.6 18.9 %collective-permute-start.40 = (bf16[4,48,1920]{2,1,0:T(8,128)(2,1)S(1)}, bf16[4,48,1920]{2,1,0:T(8,128)(2,1)S(1)}, u32[]{:S(2)}, u32[]{:S(2)}) collective-permute-start(bf16[4,48,1920]{2,1,0:T(8,128)(2,1)S(1)} %copy-done.22), channel_id=1, source_target_pairs={{0,2},{2,0},{4,6},{6,4},{8,10},{10,8},{12,14},{14,12},{16,18},{18,... | collective-permute-start | bytes 2211848 | tf_op jit(solution)/shard_map/ppermute | solution.py:643
  396.9 18.6 %collective-permute-start.41 = (bf16[4,48,1920]{2,1,0:T(8,128)(2,1)S(1)}, bf16[4,48,1920]{2,1,0:T(8,128)(2,1)S(1)}, u32[]{:S(2)}, u32[]{:S(2)}) collective-permute-start(bf16[4,48,1920]{2,1,0:T(8,128)(2,1)S(1)} %copy-done.21), channel_id=1, source_target_pairs={{0,4},{2,6},{4,0},{6,2},{8,12},{10,14},{12,8},{14,10},{16,20},{18,... | collective-permute-start | bytes 2211848 | tf_op jit(solution)/shard_map/ppermute | solution.py:643
  400.5 23.2 %collective-permute-start.55 = (f32[24,1536]{1,0:T(8,128)S(1)}, f32[24,1536]{1,0:T(8,128)S(1)}, u32[]{:S(2)}, u32[]{:S(2)}) collective-permute-start(f32[24,1536]{1,0:T(8,128)S(1)} %get-tuple-element.237), channel_id=1, source_target_pairs={{0,1},{1,0},{2,3},{3,2},{4,5},{5,4},{6,7},{7,6},{8,9},{9,8},{10,11... | collective-permute-start | bytes 442376 | tf_op jit(solution)/shard_map/ppermute | solution.py:647
  (90 other events, 532.1 us)
where the time goes:
time: 487 us; the launch traced here: 478 us
  Pallas kernels  261 us (54%)
  waiting for transfers between devices  86 us (18%)
  starting transfers between devices  59.7 us (12%)
  local copies, waits for them, and re-layouts  49.4 us (10%)
  other arithmetic  18.9 us (4%)
    pallas_call x31, Pallas kernels, call(): pl.pallas_call(inner, **common)  261 us
    ppermute x42, waiting for transfers between devices, clip_swap(): return lax.ppermute(values, 'clip', [(i, i ^ bits) for i in range(count)])  70.1 us
    ppermute x42, starting transfers between devices, clip_swap(): return lax.ppermute(values, 'clip', [(i, i ^ bits) for i in range(count)])  57.7 us
    unnamed x124, local copies, waits for them, and re-layouts  29.6 us
    ppermute x14, waiting for transfers between devices, core_swap(): return lax.ppermute(values, 'frame', [(0, 1), (1, 0)])  15.9 us
  transfers between devices with their start and end apart: 56, of which 26 were waited for; matrix products, arithmetic and copies ran while one was open for 8% of the time, Pallas kernels for 38%

commit v1 on v0

--- a/solution.py
+++ b/solution.py
@@ -13,6 +13,7 @@
 BRAIN = jnp.bfloat16
 LANES = 128
 BLOCKS = 16
+RATE = 1e9
 VMEM_BYTES = 56 * 1024 * 1024
 
 
@@ -63,57 +64,80 @@
     return (lane == head).astype(FLOAT).astype(BRAIN)
 
 
-def load_columns(core, mine, other, held, sems):
+def column_copies(core, mine, other, held, sems):
     half = held.shape[1] // 2
-    first = pltpu.make_async_copy(
-        mine.at[:, :half], held.at[:, pl.ds(pl.multiple_of(core * half, LANES), half)], sems.at[0]
-    )
-    second = pltpu.make_async_copy(
-        other.at[:, :half], held.at[:, pl.ds(pl.multiple_of((1 - core) * half, LANES), half)], sems.at[1]
-    )
-    first.start()
-    second.start()
-    return first, second
-
-
-def load_mlp(core, mine, other, up, down, sems):
+    copies = []
+    for n, (source, slot) in enumerate(((mine, core), (other, 1 - core))):
+        target = held.at[:, pl.ds(pl.multiple_of(slot * half, LANES), half)]
+        copies.append(pltpu.make_async_copy(source.at[:, :half], target, sems.at[n]))
+    return copies
+
+
+def mlp_copies(core, mine, other, up, down, sems):
     cut = up.shape[2]
-    copies = []
+    ups, downs = [], []
     for k, (source, slot) in enumerate(((mine, core), (other, 1 - core))):
         for t in (0, 1):
-            copies.append(
-                pltpu.make_async_copy(source.at[:, t * cut : (t + 1) * cut], up.at[2 * slot + t], sems.at[3 * k + t])
-            )
-        copies.append(pltpu.make_async_copy(source.at[:, 2 * cut :], down.at[:, slot], sems.at[3 * k + 2]))
-    for copy in copies:
-        copy.start()
-    return copies
-
-
-def wait_all(*copies):
-    for group in copies:
-        for copy in group:
+            part = source.at[:, t * cut : (t + 1) * cut]
+            ups.append(pltpu.make_async_copy(part, up.at[2 * slot + t], sems.at[3 * k + t]))
+        downs.append(pltpu.make_async_copy(source.at[:, 2 * cut :], down.at[:, slot], sems.at[3 * k + 2]))
+    return ups, downs
+
+
+def start_first(copies):
+    @pl.when(pl.program_id(0) == 0)
+    def _():
+        for copy in copies:
+            copy.start()
+
+
+def wait_first(copies):
+    @pl.when(pl.program_id(0) == 0)
+    def _():
+        for copy in copies:
             copy.wait()
 
 
-def time_mix_kernel(own, info, tokens, vectors, w_mine, w_other, q_out, k_out, v_out, low_out, held, sems):
+def merged(ref):
+    return ref[...].reshape(ref.shape[0] * ref.shape[1], ref.shape[2])
+
+
+def store(ref, value):
+    ref[...] = value.astype(ref.dtype).reshape(ref.shape)
+
+
+def marks(count, rows, low, high):
+    index = row_index((count * rows, 1))
+    found = (index >= low) & (index < high)
+    for n in range(1, count):
+        found = found | ((index >= n * rows + low) & (index < n * rows + high))
+    return found
+
+
+def time_mix_kernel(own_steps, info, tokens, vectors, w_mine, w_other, q_out, k_out, v_out, low_out, held, sems):
     step = pl.program_id(0)
     width = tokens.shape[-1]
 
-    @pl.when(step == 0)
-    def _():
-        wait_all(load_columns(info[0], w_mine, w_other, held, sems))
-
-    unit, _ = unit_of(tokens[0].astype(FLOAT))
+    copies = column_copies(info[0], w_mine, w_other, held, sems)
+    start_first(copies)
+    unit, _ = unit_of(merged(tokens).astype(FLOAT))
     low = (unit * vectors[0:1] + vectors[1:2]).astype(BRAIN)
-    k_out[0] = nn(low, held[:, width : 2 * width]).astype(BRAIN)
-    v_out[0] = (nn(low, held[:, 2 * width :]) + vectors[3:4]).astype(BRAIN)
-
-    @pl.when(step < own)
+    wait_first(copies)
+    store(k_out, nn(low, held[:, width : 2 * width]))
+    store(v_out, nn(low, held[:, 2 * width :]) + vectors[3:4])
+
+    @pl.when(step < own_steps)
     def _():
         queries = (nn(low, held[:, :width]) + vectors[2:3]).astype(BRAIN)
-        q_out[0] = queries * jnp.asarray(HEAD_DIM ** (-0.5), BRAIN)
-        low_out[0] = low
+        store(q_out, queries * jnp.asarray(HEAD_DIM ** (-0.5), BRAIN))
+        store(low_out, low)
+
+
+def tree_sum(values):
+    values = list(values)
+    while len(values) > 1:
+        values = [a + b for a, b in zip(values[::2], values[1::2])] + values[len(values) & ~1 :]
+    return values[0]
 
 
 def attention_kernel(
@@ -123,63 +147,66 @@
 ):
     step = pl.program_id(0)
     frames = k_in.shape[0]
-    rows, width = tokens.shape[1:]
+    count, rows, width = tokens.shape
     core = info[0]
 
-    @pl.when(step == 0)
-    def _():
-        wait_all(load_columns(core, sw_mine, sw_other, held, sems))
-
+    copies = column_copies(core, sw_mine, sw_other, held, sems)
+    start_first(copies)
     mapping = head_map(width)
     spread = head_spread(width)
-    queries = q_in[0]
-    scores = [nn(queries * k_in[g], mapping) for g in range(frames)]
-    top = functools.reduce(jnp.maximum, scores)
-    powers = [jnp.exp(s - top) for s in scores]
-    scale = 1.0 / sum(powers)
-    total = jnp.zeros((rows, width), FLOAT)
-    for g in range(frames):
-        prob = (powers[g] * scale).astype(BRAIN)
-        prob_out[0, g] = prob
-        total = total + nn(prob, spread) * v_in[g].astype(FLOAT)
-    attended = total.astype(BRAIN)
-    att_out[0] = attended
-    place = row_index((rows, 1)) < places_here
-    base = tokens[0].astype(FLOAT)
+    for n in range(count):
+        queries = q_in[n]
+        scores = [nn(queries * k_in[g], mapping) for g in range(frames)]
+        top = functools.reduce(jnp.maximum, scores)
+        powers = [jnp.exp(s - top) for s in scores]
+        scale = 1.0 / sum(powers)
+        parts = []
+        for g in range(frames):
+            prob = (powers[g] * scale).astype(BRAIN)
+            prob_out[n, g] = prob
+            parts.append(nn(prob, spread).astype(BRAIN) * v_in[g])
+        att_out[n] = tree_sum(parts)
+    wait_first(copies)
+    attended = merged(att_out)
+    place = marks(count, rows, 0, places_here)
+    base = merged(tokens).astype(FLOAT)
     after = jnp.where(place, base + (nn(attended, held[:, 4 * width :]) + vectors[4:5]), base)
-    after_out[0] = after
+    store(after_out, after)
     unit, _ = unit_of(after)
     low = (unit * vectors[5:6] + vectors[6:7]).astype(BRAIN)
-    low_out[0] = low
-    mixed_out[0, :, :width] = (
-        (nn(low, held[:, :width]) + vectors[7:8]).astype(BRAIN) * jnp.asarray(HEAD_DIM ** (-0.5), BRAIN)
-    )
-    mixed_out[0, :, width : 2 * width] = nn(low, held[:, width : 2 * width]).astype(BRAIN)
-    mixed_out[0, :, 2 * width :] = (nn(low, held[:, 2 * width : 3 * width]) + vectors[8:9]).astype(BRAIN)
+    store(low_out, low)
+    shape = (count, rows, width)
+    queries = (nn(low, held[:, :width]) + vectors[7:8]).astype(BRAIN) * jnp.asarray(HEAD_DIM ** (-0.5), BRAIN)
+    mixed_out[:, :, :width] = queries.reshape(shape)
+    mixed_out[:, :, width : 2 * width] = nn(low, held[:, width : 2 * width]).astype(BRAIN).reshape(shape)
+    mixed_out[:, :, 2 * width :] = (
+        (nn(low, held[:, 2 * width : 3 * width]) + vectors[8:9]).astype(BRAIN).reshape(shape)
+    )
     lane = lax.broadcasted_iota(jnp.int32, (1, LANES), 1)
     masks = [(lane // HEAD_DIM == e).astype(FLOAT).astype(BRAIN) for e in (0, 1)]
-    key_ok = lax.broadcasted_iota(jnp.int32, (1, rows), 1) <= places_here
-    for pair in range(width // LANES):
-        at = pair * LANES
-        q2 = mixed_out[0, :, at : at + LANES]
-        k2 = mixed_out[0, :, width + at : width + at + LANES]
-        v2 = mixed_out[0, :, 2 * width + at : 2 * width + at + LANES]
-        result = []
-        for e in (0, 1):
-            logits = jnp.where(key_ok, nt(q2 * masks[e], k2), -1e30)
-            power = jnp.exp(logits - jnp.max(logits, axis=-1, keepdims=True))
-            prob = (power * (1.0 / jnp.sum(power, axis=-1, keepdims=True))).astype(BRAIN)
-            sprob_out[0, 2 * pair + e] = prob
-            result.append(nn(prob, v2))
-        satt_out[0, :, at : at + LANES] = jnp.where(lane < HEAD_DIM, result[0], result[1]).astype(BRAIN)
-    spatial = nn(satt_out[0], held[:, 3 * width : 4 * width]) + vectors[9:10]
-    places_out[0] = jnp.where(place, after, 0.0) + spatial
+    key_ok = row_index((rows, 1)) <= places_here
+    for n in range(count):
+        for pair in range(width // LANES):
+            at = pair * LANES
+            q2 = mixed_out[n, :, at : at + LANES]
+            k2 = mixed_out[n, :, width + at : width + at + LANES]
+            v2 = mixed_out[n, :, 2 * width + at : 2 * width + at + LANES]
+            result = []
+            for e in (0, 1):
+                logits = jnp.where(key_ok, nt(k2, q2 * masks[e]), -1e30)
+                power = jnp.exp(logits - jnp.max(logits, axis=0, keepdims=True))
+                prob = (power * (1.0 / jnp.sum(power, axis=0, keepdims=True))).astype(BRAIN)
+                sprob_out[n, 2 * pair + e] = prob
+                result.append(tn(prob, v2))
+            satt_out[n, :, at : at + LANES] = jnp.where(lane < HEAD_DIM, result[0], result[1]).astype(BRAIN)
+    spatial = nn(merged(satt_out), held[:, 3 * width : 4 * width]) + vectors[9:10]
+    store(places_out, jnp.where(place, after, 0.0) + spatial)
 
     @pl.when(step == 0)
     def _():
         class_out[...] = begin[...]
 
-    class_row = column_sum(jnp.where(row_index((rows, 1)) == places_here, spatial, 0.0))
+    class_row = column_sum(jnp.where(marks(count, rows, places_here, places_here + 1), spatial, 0.0))
     class_out[0:1] = class_out[0:1] + class_row
 
 
@@ -195,116 +222,129 @@
     out, low_out, hidden_out, feed_out, before_out, rows_out, sums, slopes, up, down, sems,
 ):
     step = pl.program_id(0)
-    rows, width = places.shape[1:]
+    count, rows, width = places.shape
     core = info[0]
 
+    ups, downs = mlp_copies(core, w_mine, w_other, up, down, sems)
+    start_first(ups + downs)
+
     @pl.when(step == 0)
     def _():
         sums[...] = jnp.zeros_like(sums)
-        wait_all(load_mlp(core, w_mine, w_other, up, down, sems))
 
     class_mid = class_row[0:1] + (class_own[0:1] + class_far[0:1]) * all_frames ** (-0.5)
-    class_at = row_index((rows, 1)) == places_here
-    is_class = class_at & (step == pl.num_programs(0) - 1)
-    kept = jnp.logical_not(class_at & (info[1] == 0))
-    values = jnp.where(is_class, class_mid, places[0])
+    last = (count - 1) * rows + places_here
+    is_class = (row_index((count * rows, 1)) == last) & (step == pl.num_programs(0) - 1)
+    kept = jnp.logical_not(marks(count, rows, places_here, places_here + 1) & (info[1] == 0))
+    values = jnp.where(is_class, class_mid, merged(places))
     unit, inverse = unit_of(values)
     low = (unit * vectors[10:11] + vectors[11:12]).astype(BRAIN)
-    low_out[0] = low
-    feed = jnp.zeros((rows, width), FLOAT)
+    store(low_out, low)
+    feed = jnp.zeros((count * rows, width), FLOAT)
     chunks = hidden_out.shape[-1] // width
     per = down.shape[0] // chunks
+    wait_first(ups)
     for j in range(chunks):
         before = nn(low, up[j].reshape(width, width)) + bias[j : j + 1]
         hidden, slope = gelu_parts(before)
         hidden = hidden.astype(BRAIN)
-        hidden_out[0, :, j * width : (j + 1) * width] = hidden
+        hidden_out[:, :, j * width : (j + 1) * width] = hidden.reshape(count, rows, width)
         slopes[j] = slope
+        if j == 0:
+            wait_first(downs)
         feed = feed + nn(hidden, down[j * per : (j + 1) * per].reshape(width, width))
-    out[0] = ((values + (feed + vectors[12:13])) * alive[0]).astype(BRAIN)
-
-    row_grad = grads[0].astype(FLOAT) * alive[0]
+    store(out, (values + (feed + vectors[12:13])) * alive[0])
+
+    row_grad = merged(grads).astype(FLOAT) * alive[0]
     feed_grad = row_grad.astype(BRAIN)
     feed_kept = jnp.where(kept, row_grad, 0.0).astype(BRAIN)
-    feed_out[0] = feed_kept
+    store(feed_out, feed_kept)
     sums[2:3] = sums[2:3] + column_sum(feed_kept.astype(FLOAT))
-    upstream = jnp.zeros((rows, width), FLOAT)
+    upstream = jnp.zeros((count * rows, width), FLOAT)
     for j in range(chunks):
         hidden_grad = nt(feed_grad, down[j * per : (j + 1) * per].reshape(width, width))
         before_grad = (hidden_grad * slopes[j]).astype(BRAIN)
         before_kept = jnp.where(kept, before_grad.astype(FLOAT), 0.0)
-        before_out[0, :, j * width : (j + 1) * width] = before_kept.astype(BRAIN)
+        before_out[:, :, j * width : (j + 1) * width] = before_kept.astype(BRAIN).reshape(count, rows, width)
         sums[3 + j : 4 + j] = sums[3 + j : 4 + j] + column_sum(before_kept)
         upstream = upstream + nt(before_grad, up[j].reshape(width, width))
-    rows_out[0] = row_grad + norm_back(unit, inverse, vectors[10:11], upstream)
+    store(rows_out, row_grad + norm_back(unit, inverse, vectors[10:11], upstream))
     upstream = jnp.where(kept, upstream, 0.0)
     sums[0:1] = sums[0:1] + column_sum(upstream * unit)
     sums[1:2] = sums[1:2] + column_sum(upstream)
 
 
 def space_back_kernel(
-    places_here, all_frames, info, rows_grad, class_grad, after, mixed, sprob, vectors, begin,
+    places_here, all_frames, info, rows_grad, class_grad, after, mixed, sprob, satt, vectors, begin,
     sw_mine, sw_other,
     branch_out, mixed_out, after_out, time_out, att_out, sums, held, sems,
 ):
     step = pl.program_id(0)
-    rows, width = after.shape[1:]
+    count, rows, width = after.shape
     core = info[0]
 
+    copies = column_copies(core, sw_mine, sw_other, held, sems)
+    start_first(copies)
+
     @pl.when(step == 0)
     def _():
         sums[...] = begin[...]
-        wait_all(load_columns(core, sw_mine, sw_other, held, sems))
-
-    index = row_index((rows, 1))
-    place = index < places_here
-    class_at = index == places_here
+
+    place = marks(count, rows, 0, places_here)
+    class_at = marks(count, rows, places_here, places_here + 1)
     offset = places_here % 16
     share = class_grad[0, offset : offset + 1] * all_frames ** (-0.5)
-    direct = jnp.where(place, rows_grad[0], 0.0)
+    direct = jnp.where(place, merged(rows_grad), 0.0)
     branch = jnp.where(class_at, share, direct).astype(BRAIN)
-    branch_out[0] = branch
+    store(branch_out, branch)
     sums[4:5] = sums[4:5] + column_sum(branch.astype(FLOAT))
+    unit, inverse = unit_of(merged(after))
+    wait_first(copies)
     att_grad = nt(branch, held[:, 3 * width : 4 * width]).astype(BRAIN)
+    store(att_out, att_grad)
+    spread = head_spread(width)
     lane = lax.broadcasted_iota(jnp.int32, (1, LANES), 1)
     masks = [(lane // HEAD_DIM == e).astype(FLOAT).astype(BRAIN) for e in (0, 1)]
-    for pair in range(width // LANES):
-        at = pair * LANES
-        a2 = att_grad[:, at : at + LANES]
-        q2 = mixed[0, :, at : at + LANES]
-        k2 = mixed[0, :, width + at : width + at + LANES]
-        v2 = mixed[0, :, 2 * width + at : 2 * width + at + LANES]
-        queries, key_rows, value_rows = [], [], []
-        for e in (0, 1):
-            prob = sprob[0, 2 * pair + e]
-            wide = prob.astype(FLOAT)
-            prob_grad = nt(a2 * masks[e], v2)
-            weighted = wide * prob_grad
-            rowdot = jnp.sum(weighted, axis=-1, keepdims=True)
-            score = (weighted - wide * rowdot).astype(BRAIN)
-            queries.append(nn(score, k2))
-            key_rows.append(tn(score, q2))
-            value_rows.append(tn(prob, a2))
-        left = lane < HEAD_DIM
-        q_grad = (jnp.where(left, queries[0], queries[1]) * HEAD_DIM ** (-0.5)).astype(BRAIN)
-        v_grad = jnp.where(left, value_rows[0], value_rows[1]).astype(BRAIN)
-        mixed_out[0, :, at : at + LANES] = q_grad
-        mixed_out[0, :, width + at : width + at + LANES] = jnp.where(left, key_rows[0], key_rows[1]).astype(BRAIN)
-        mixed_out[0, :, 2 * width + at : 2 * width + at + LANES] = v_grad
-    sums[2:3] = sums[2:3] + column_sum(mixed_out[0, :, :width].astype(FLOAT))
-    sums[3:4] = sums[3:4] + column_sum(mixed_out[0, :, 2 * width :].astype(FLOAT))
-    upstream = nt(mixed_out[0], held[:, : 3 * width])
-    unit, inverse = unit_of(after[0])
+    left = lane < HEAD_DIM
+    for n in range(count):
+        product = att_out[n].astype(FLOAT) * satt[n].astype(FLOAT)
+        high = product.astype(BRAIN)
+        rowdots = nt(spread, high) + nt(spread, (product - high.astype(FLOAT)).astype(BRAIN))
+        for pair in range(width // LANES):
+            at = pair * LANES
+            a2 = att_out[n, :, at : at + LANES]
+            q2 = mixed[n, :, at : at + LANES]
+            k2 = mixed[n, :, width + at : width + at + LANES]
+            v2 = mixed[n, :, 2 * width + at : 2 * width + at + LANES]
+            queries, key_rows, value_rows = [], [], []
+            for e in (0, 1):
+                head = 2 * pair + e
+                prob = sprob[n, head]
+                prob_grad = nt(v2, a2 * masks[e])
+                score = (prob.astype(FLOAT) * (prob_grad - rowdots[head : head + 1])).astype(BRAIN)
+                queries.append(tn(score, k2))
+                key_rows.append(nn(score, q2))
+                value_rows.append(nn(prob, a2))
+            q_grad = (jnp.where(left, queries[0], queries[1]) * HEAD_DIM ** (-0.5)).astype(BRAIN)
+            k_grad = jnp.where(left, key_rows[0], key_rows[1]).astype(BRAIN)
+            v_grad = jnp.where(left, value_rows[0], value_rows[1]).astype(BRAIN)
+            mixed_out[n, :, at : at + LANES] = q_grad
+            mixed_out[n, :, width + at : width + at + LANES] = k_grad
+            mixed_out[n, :, 2 * width + at : 2 * width + at + LANES] = v_grad
+    mixed_grad = merged(mixed_out)
+    sums[2:3] = sums[2:3] + column_sum(mixed_grad[:, :width].astype(FLOAT))
+    sums[3:4] = sums[3:4] + column_sum(mixed_grad[:, 2 * width :].astype(FLOAT))
+    upstream = nt(mixed_grad, held[:, : 3 * width])
     inner = norm_back(unit, inverse, vectors[5:6], upstream)
     sums[0:1] = sums[0:1] + column_sum(upstream * unit)
     sums[1:2] = sums[1:2] + column_sum(upstream)
     sums[6:7] = sums[6:7] + column_sum(jnp.where(class_at, inner, 0.0))
     after_grad = jnp.where(place, direct + inner, 0.0)
-    after_out[0] = after_grad
+    store(after_out, after_grad)
     low = after_grad.astype(BRAIN)
-    time_out[0] = low
+    store(time_out, low)
     sums[5:6] = sums[5:6] + column_sum(low.astype(FLOAT))
-    att_out[0] = nt(low, held[:, 4 * width :]).astype(BRAIN)
+    store(att_out, nt(low, held[:, 4 * width :]))
 
 
 def time_back_kernel(q_in, k_in, v_in, prob_in, att_in, q_out, own_out, far_out):
@@ -329,20 +369,20 @@
             ]
             rowdot = sum(weighted)
             scores += [(weighted[g] - wide[g] * rowdot).astype(BRAIN) for g in range(frames)]
-        score_wide = nn(jnp.concatenate(scores, axis=0), spread)
-        prob_wide = nn(jnp.concatenate(probs, axis=0), spread)
+        score_wide = nn(jnp.concatenate(scores, axis=0), spread).astype(BRAIN)
+        prob_wide = nn(jnp.concatenate(probs, axis=0), spread).astype(BRAIN)
 
         def part(array, f, g):
             return array[(f * frames + g) * size : (f * frames + g + 1) * size]
 
+        keys = [k_in[g, at] for g in range(frames)]
         for f in range(own):
-            total = sum(part(score_wide, f, g) * k_in[g, at].astype(FLOAT) for g in range(frames))
-            q_out[f, at] = (total * HEAD_DIM ** (-0.5)).astype(BRAIN)
-        queries = [q_in[f, at].astype(FLOAT) for f in range(own)]
-        wide_att = [a.astype(FLOAT) for a in att]
+            total = tree_sum(part(score_wide, f, g) * keys[g] for g in range(frames))
+            q_out[f, at] = total * jnp.asarray(HEAD_DIM ** (-0.5), BRAIN)
+        queries = [q_in[f, at] for f in range(own)]
         for g in range(frames):
-            key_grad = sum(part(score_wide, f, g) * queries[f] for f in range(own)).astype(BRAIN)
-            value_grad = sum(part(prob_wide, f, g) * wide_att[f] for f in range(own)).astype(BRAIN)
+            key_grad = tree_sum(part(score_wide, f, g) * queries[f] for f in range(own))
+            value_grad = tree_sum(part(prob_wide, f, g) * att[f] for f in range(own))
             if g < own:
                 own_out[0, g, at] = key_grad
                 own_out[1, g, at] = value_grad
@@ -358,64 +398,129 @@
     step = pl.program_id(0)
     width = tokens.shape[-1]
 
+    copies = column_copies(info[0], w_mine, w_other, held, sems)
+    start_first(copies)
+
     @pl.when(step == 0)
     def _():
         sums[...] = jnp.zeros_like(sums)
-        wait_all(load_columns(info[0], w_mine, w_other, held, sems))
-
-    sums[2:3] = sums[2:3] + column_sum(mixed[0, :, :width].astype(FLOAT))
-    sums[3:4] = sums[3:4] + column_sum(mixed[0, :, 2 * width :].astype(FLOAT))
-    upstream = nt(mixed[0], held[...])
-    unit, inverse = unit_of(tokens[0].astype(FLOAT))
-    token_out[0] = after_grad[0] + norm_back(unit, inverse, vectors[0:1], upstream)
+
+    mixed_grad = merged(mixed)
+    sums[2:3] = sums[2:3] + column_sum(mixed_grad[:, :width].astype(FLOAT))
+    sums[3:4] = sums[3:4] + column_sum(mixed_grad[:, 2 * width :].astype(FLOAT))
+    unit, inverse = unit_of(merged(tokens).astype(FLOAT))
+    wait_first(copies)
+    upstream = nt(mixed_grad, held[...])
+    store(token_out, merged(after_grad) + norm_back(unit, inverse, vectors[0:1], upstream))
     sums[0:1] = sums[0:1] + column_sum(upstream * unit)
     sums[1:2] = sums[1:2] + column_sum(upstream)
 
 
-def time_outer_kernel(info, left, right, sums, out):
-    half = right.shape[1]
-    out[:, :half] = tn(left[...], right[...]).astype(BRAIN)
-    out[:, half:] = sums[...].astype(BRAIN)
-
-
-def space_outer_kernel(info, low, mixed, att, branch, time_att, time_grad, out):
-    width = low.shape[1]
-    half = out.shape[1]
-    rest = 3 * width - half
-
-    @pl.when(info[0] == 0)
-    def _():
-        out[...] = tn(low[...], mixed[:, :half]).astype(BRAIN)
-
-    @pl.when(info[0] == 1)
-    def _():
-        out[:, :rest] = tn(low[...], mixed[:, half:]).astype(BRAIN)
-        out[:, rest : rest + width] = tn(att[...], branch[...]).astype(BRAIN)
-        out[:, rest + width :] = tn(time_att[...], time_grad[...]).astype(BRAIN)
-
-
-def mlp_outer_kernel(info, low, before, hidden, feed, mine, other):
+def mixed_grad_kernel(queries, own, far, out):
+    width = queries.shape[2]
+    out[:, :, :width] = queries[...]
+    out[:, :, width : 2 * width] = (own[0].astype(FLOAT) + far[0].astype(FLOAT)).astype(BRAIN)
+    out[:, :, 2 * width :] = (own[1].astype(FLOAT) + far[1].astype(FLOAT)).astype(BRAIN)
+
+
+def sums_kernel(time_sums, space_sums, mlp_sums, bias, out, lines):
+    lines[...] = jnp.zeros_like(lines)
+    lines[0:4] = time_sums[0:4]
+    lines[4:5] = space_sums[5:6]
+    lines[5:10] = space_sums[0:5]
+    lines[10:13] = mlp_sums[0:3]
+    count = bias.shape[1]
+    place = lax.broadcasted_iota(jnp.int32, (count, LANES), 1) == row_index((count, LANES)) + 13
+    spread = lax.dot_general(
+        bias[...], place.astype(FLOAT), (((1,), (0,)), ((), ())), preferred_element_type=FLOAT,
+        precision=lax.Precision.HIGHEST,
+    )
+    out[...] = lines[...].T + spread
+
+
+def halves_kernel(left, right, left_out, right_out):
+    left_out[...] = left[...]
+    right_out[...] = right[...]
+
+
+def share_rows(info, value, mine, other, at=slice(None)):
+    value = value.reshape(mine.shape[0], 2, mine.shape[1], value.shape[-1])
+    first = info[0] == 0
+    mine[:, :, at] = jnp.where(first, value[:, 0], value[:, 1]).astype(BRAIN)
+    other[:, :, at] = jnp.where(first, value[:, 1], value[:, 0]).astype(BRAIN)
+
+
+def time_outer_kernel(info, left, right, sums, mine, other):
     step = pl.program_id(0)
-    blocks, total, width = mine.shape
-    cut = total // 4
-    per = blocks // pl.num_programs(0)
-    part = tn(low[...], before[...]).astype(BRAIN).reshape(blocks, cut, width)
-    at = pl.ds(pl.multiple_of((step % 2) * cut, 16), cut)
-    is_mine = step // 2 == info[0]
-
-    @pl.when(is_mine)
-    def _():
-        mine[:, at] = part
-
-    @pl.when(jnp.logical_not(is_mine))
-    def _():
-        other[:, at] = part
-
+    width = left.shape[1]
+
+    for n in range(3):
+
+        @pl.when(step == n)
+        def _():
+            share_rows(info, tn(left[...], right[...]), mine, other, slice(n * width, (n + 1) * width))
+
+    @pl.when(step == 0)
+    def _():
+        share_rows(info, sums[...], mine, other, slice(3 * width, 3 * width + sums.shape[1]))
+
+
+def space_outer_kernel(info, low, mixed, att, branch, time_att, time_grad, mine, other):
+    step = pl.program_id(0)
+
+    @pl.when(step < 3)
+    def _():
+        share_rows(info, tn(low[...], mixed[...]), mine, other)
+
+    @pl.when(step == 3)
+    def _():
+        share_rows(info, tn(att[...], branch[...]), mine, other)
+
+    @pl.when(step == 4)
+    def _():
+        share_rows(info, tn(time_att[...], time_grad[...]), mine, other)
+
+
+def mlp_outer_kernel(info, low, before, hidden, feed, mine, other, turned, ups, downs, sems):
+    step = pl.program_id(0)
+    steps = ups.shape[0]
+    blocks, cut, width = ups.shape[1:]
+    per = downs.shape[2]
+
+    @pl.when(step == 0)
+    def _():
+        turned[...] = low[...].T
+
+    ups[step] = nn(turned[...], before[...]).astype(BRAIN).reshape(blocks, cut, width)
     value = tn(hidden[...], feed[...]).astype(BRAIN).reshape(per, 2, 2 * cut, width)
-    first = info[0] == 0
-    rows = pl.ds(pl.multiple_of(step * per, per), per)
-    mine[rows, 2 * cut :] = jnp.where(first, value[:, 0], value[:, 1])
-    other[rows, 2 * cut :] = jnp.where(first, value[:, 1], value[:, 0])
+    downs[step, 0] = value[:, 0]
+    downs[step, 1] = value[:, 1]
+
+    for n in range(steps):
+        targets = (mine, other)
+        for k, slot in ((0, info[0]), (1, 1 - info[0])):
+            up_copy = pltpu.make_async_copy(
+                ups.at[n], targets[k].at[:, (n % 2) * cut : (n % 2 + 1) * cut], sems.at[0, n]
+            )
+            down_copy = pltpu.make_async_copy(
+                downs.at[n, slot], targets[k].at[n * per : (n + 1) * per, 2 * cut :], sems.at[1 + k, n]
+            )
+
+            @pl.when((step == n) & (slot == n // 2))
+            def _():
+                up_copy.start()
+
+            @pl.when(step == n)
+            def _():
+                down_copy.start()
+
+            @pl.when((step == steps - 1) & (slot == n // 2))
+            def _():
+                up_copy.wait()
+
+            @pl.when(step == steps - 1)
+            def _():
+                down_copy.wait()
 
 
 def smem():
@@ -430,15 +535,15 @@
     return pl.BlockSpec(shape, lambda *_: (0,) * len(shape))
 
 
-def per_frame(shape, first=0):
-    return pl.BlockSpec((1,) + shape[1:], lambda s: (s + first,) + (0,) * (len(shape) - 1))
+def per_frame(shape, first=0, count=1):
+    return pl.BlockSpec((count,) + shape[1:], lambda s: (s + first // count,) + (0,) * (len(shape) - 1))
 
 
 def sds(shape, kind):
     return jax.ShapeDtypeStruct(shape, kind)
 
 
-def call(kernel, grid, inputs, outputs, scratch=(), flops=0, nbytes=0, deps=(), previous=(), prefetch=0):
+def call(kernel, grid, inputs, outputs, scratch=(), micros=2, deps=(), previous=(), prefetch=0):
     count = len(inputs)
     skip = len(previous) + len(deps)
 
@@ -447,10 +552,11 @@
 
     specs = [spec for spec, _ in inputs[prefetch:]] + [hbm()] * skip
     common = dict(
+        name=getattr(kernel, "func", kernel).__name__,
         out_shape=[shape for _, shape in outputs],
         compiler_params=pltpu.CompilerParams(vmem_limit_bytes=VMEM_BYTES),
         input_output_aliases={count + n: n for n in range(len(previous))},
-        cost_estimate=pl.CostEstimate(flops=1, bytes_accessed=1, transcendentals=0),
+        cost_estimate=pl.CostEstimate(flops=int(micros * RATE), bytes_accessed=1, transcendentals=0),
     )
     places = dict(grid=grid, in_specs=specs, out_specs=[spec for spec, _ in outputs], scratch_shapes=list(scratch))
     if prefetch:
@@ -462,43 +568,47 @@
 
 def time_outer(slot, left, right, sums, deps=()):
     rows, width = left.shape
-    half = right.shape[1] // 2
-    shape = (width, half + sums.shape[1])
+    wide = right.shape[1]
+    shape = (BLOCKS, width // (2 * BLOCKS), wide + sums.shape[1])
     return call(
-        time_outer_kernel, (1,),
+        time_outer_kernel, (3,),
         [
-            (None, slot),
-            (pl.BlockSpec((rows, width), lambda s, info: (0, 0)), left),
-            (pl.BlockSpec((rows, half), lambda s, info: (0, info[0])), right),
-            (pl.BlockSpec(sums.shape, lambda s, info: (0, 0)), sums),
+            (smem(), slot), (whole(left.shape), left), (pl.BlockSpec((rows, width), lambda s: (0, s)), right),
+            (whole(sums.shape), sums),
         ],
-        [(pl.BlockSpec(shape, lambda s, info: (0, 0)), sds(shape, BRAIN))],
-        flops=2 * rows * width * half, nbytes=4 * rows * (width + half), deps=deps, prefetch=1,
-    )[0]
-
-
-def space_outer(slot, *operands, deps=()):
-    rows, width = operands[0].shape
-    half = width * 5 // 2
+        [(whole(shape), sds(shape, BRAIN))] * 2, micros=8, deps=deps,
+    )
+
+
+def space_outer(slot, low, mixed, *others, deps=()):
+    rows, width = low.shape
+    shape = (BLOCKS, width // (2 * BLOCKS), width)
+    moving = pl.BlockSpec((rows, width), lambda s: (0, jnp.minimum(s, 2)))
     return call(
-        space_outer_kernel, (1,),
-        [(smem(), slot)] + [(whole(v.shape), v) for v in operands],
-        [(whole((width, half)), sds((width, half), BRAIN))],
-        flops=2 * rows * width * half, nbytes=4 * rows * (width + half), deps=deps,
-    )[0]
+        space_outer_kernel, (5,),
+        [(smem(), slot), (whole(low.shape), low), (moving, mixed)] + [(whole(v.shape), v) for v in others],
+        [(pl.BlockSpec(shape, lambda s: (0, 0, s)), sds(shape[:2] + (5 * width,), BRAIN))] * 2, micros=12, deps=deps,
+    )
 
 
 def mlp_outer(slot, low, before, hidden, feed, deps=()):
     rows, width = low.shape
     wide = hidden.shape[1]
-    shape = (BLOCKS, 4 * (width // BLOCKS), width)
+    cut = width // BLOCKS
+    shape = (BLOCKS, 4 * cut, width)
     fixed = pl.BlockSpec((rows, width), lambda s, info: (0, 0))
     moving = pl.BlockSpec((rows, width), lambda s, info: (0, s))
     return call(
         mlp_outer_kernel, (wide // width,),
         [(None, slot), (fixed, low), (moving, before), (moving, hidden), (fixed, feed)],
-        [(pl.BlockSpec(shape, lambda s, info: (0, 0, 0)), sds(shape, BRAIN))] * 2,
-        flops=4 * rows * width * wide, nbytes=4 * rows * (wide + width), deps=deps, prefetch=1,
+        [(hbm(), sds(shape, BRAIN))] * 2,
+        [
+            pltpu.VMEM((width, rows), BRAIN),
+            pltpu.VMEM((wide // width, BLOCKS, cut, width), BRAIN),
+            pltpu.VMEM((wide // width, 2, BLOCKS * width // wide, 2 * cut, width), BRAIN),
+            pltpu.SemaphoreType.DMA((3, wide // width)),
+        ],
+        micros=21, deps=deps, prefetch=1,
     )
 
 
@@ -665,7 +775,7 @@
         shape = (len(pieces),) + pieces[0].shape
         return call(
             stack_kernel, (1,), [(whole(v.shape), v) for v in pieces], [(whole(shape), sds(shape, BRAIN))],
-            nbytes=4 * len(pieces) * pieces[0].size, deps=deps,
+            micros=3, deps=deps,
         )[0]
 
     def depth_direct(self, own, deps):
@@ -681,9 +791,13 @@
     def plane_step(self, o4, deps):
         rx = self.swap(o4, 1)
         ry = self.swap(o4, 2)
-        if deps:
-            rx, ry = gate(rx, deps), gate(ry, deps)
-        return rx, ry, rx[:2], ry[2:]
+        half = (2,) + o4.shape[1:]
+        first = pl.BlockSpec(half, lambda s: (0, 0, 0))
+        second = pl.BlockSpec(half, lambda s: (1, 0, 0))
+        sx, sy = call(
+            halves_kernel, (1,), [(first, rx), (second, ry)], [(whole(half), sds(half, BRAIN))] * 2, deps=deps
+        )
+        return rx, ry, sx, sy
 
     def diagonal_step(self, o4, planes, deps):
         rx, ry, sx, sy = planes
@@ -691,7 +805,7 @@
         shape = (self.clips,) + o4.shape[1:]
         return call(
             assemble_kernel, (1,), [(smem(), self.info)] + [(whole(v.shape), v) for v in pieces],
-            [(whole(shape), sds(shape, BRAIN))], nbytes=16 * o4.size, deps=deps,
+            [(whole(shape), sds(shape, BRAIN))], micros=3, deps=deps,
         )[0]
 
     def reduce_first(self, mine, far, deps):
@@ -708,7 +822,7 @@
                 (one(lambda s: jnp.maximum(s - 2, 0)), sds((2,) + block, BRAIN)),
                 each, each, each,
             ],
-            nbytes=6 * mine.size, deps=deps,
+            micros=20, deps=deps,
         )
 
     def reduce_second(self, near_x, near_y, to_y, to_x, deps):
@@ -722,7 +836,7 @@
                 (each, near_x), (each, near_y), (one(lambda s: jnp.minimum(s, 1)), from_y),
                 (one(lambda s: jnp.maximum(s - 2, 0)), from_x),
             ],
-            [(each, sds(near_x.shape, BRAIN))] * 2, nbytes=10 * near_x.size, deps=deps,
+            [(each, sds(near_x.shape, BRAIN))] * 2, micros=20, deps=deps,
         )
 
     def reduce_third(self, own, near_x, near_y, deps):
@@ -732,14 +846,14 @@
             reduce_third_kernel, (1,),
             [(smem(), self.info)] + [(whole(v.shape), v) for v in (own, from_x, from_y)],
             [(whole(shape), sds(shape, BRAIN)) for shape in (block, block, (2,) + block)],
-            nbytes=8 * own.size, deps=deps,
+            micros=20, deps=deps,
         )
 
     def reduce_fourth(self, first, second, others, deps):
         come = self.swap(others, 8)
         inputs = [(whole(v.shape), v) for v in (first, second, come)]
         outs = [(whole(first.shape), sds(first.shape, kind)) for kind in (FLOAT, BRAIN)]
-        return call(reduce_fourth_kernel, (1,), inputs, outs, nbytes=8 * first.size, deps=deps)
+        return call(reduce_fourth_kernel, (1,), inputs, outs, micros=20, deps=deps)
 
     def reduce_end(self, first, second):
         return first + self.swap(second, 4).astype(FLOAT)
@@ -822,7 +936,7 @@
         )[0]
         n_vec = time_vec.shape[0] + space_vec.shape[0] + mlp_vec.shape[0]
         bias = vectors[n_vec : n_vec + bias_rows].T.reshape(bias_rows, width)
-        mlp_own = gate(mlp_own, [time_far, space_line])
+        mlp_own = gate(mlp_own, [time_mine])
         mix_deps = [space_line, mlp_own]
     else:
         everywhere = lax.all_gather(tokens, "frame", axis=0, tiled=True)
@@ -856,8 +970,10 @@
     sum_out = (whole((8, width)), sds((8, width), FLOAT))
     row_bytes = own * rows * width
     square = 2 * own * rows * width * width
-    low_out = lambda shape, first=0: (per_frame(shape, first), sds(shape, BRAIN))
-    wide_out = lambda shape, first=0: (per_frame(shape, first), sds(shape, FLOAT))
+    group = 2 if own % 2 == 0 else 1
+    frames_in = lambda array, first=0: (per_frame(array.shape, first, group), array)
+    low_out = lambda shape, first=0: (per_frame(shape, first, group), sds(shape, BRAIN))
+    wide_out = lambda shape, first=0: (per_frame(shape, first, group), sds(shape, FLOAT))
     vec_in = (whole(vectors.shape), vectors)
     pair = lambda two: [(hbm(), two[0]), (hbm(), two[1])]
     time_held = [pltpu.VMEM((width, 3 * width), BRAIN), pltpu.SemaphoreType.DMA((2,))]
@@ -868,16 +984,16 @@
         pltpu.SemaphoreType.DMA((6,)),
     ]
 
-    own_map = pl.BlockSpec((1, rows, width), lambda s: (jnp.minimum(s, own - 1), 0, 0))
+    own_map = pl.BlockSpec((group, rows, width), lambda s: (jnp.minimum(s, own // group - 1), 0, 0))
     queries, key_rows, value_rows, time_low = call(
-        functools.partial(time_mix_kernel, own), (frames,),
-        [(smem(), info), (per_frame(all_shape), all_tokens), vec_in] + pair(time_w),
+        functools.partial(time_mix_kernel, own // group), (frames // group,),
+        [(smem(), info), frames_in(all_tokens), vec_in] + pair(time_w),
         [(own_map, sds(frame_shape, BRAIN)), low_out(all_shape), low_out(all_shape), (own_map, sds(frame_shape, BRAIN))],
-        time_held, flops=5 * square, nbytes=20 * row_bytes, deps=mix_deps,
+        time_held, micros=12, deps=mix_deps,
     )
 
     if near is not None:
-        mlp_line = near.depth_direct(mlp_own, [])
+        mlp_line = near.depth_direct(mlp_own, [queries])
         space_mine = near.diagonal_step(space_line, near.plane_step(space_line, [queries, mlp_line]), [])
         space_w = join((space_mine, core_swap(space_mine)))
         mlp_line = gate(mlp_line, [space_mine])
@@ -887,9 +1003,9 @@
     kept, class_own = (), zeros
     for first, count in parts:
         outs = call(
-            functools.partial(attention_kernel, places_here), (count,),
+            functools.partial(attention_kernel, places_here), (count // group,),
             [
-                (smem(), info), (per_frame(frame_shape, first), tokens), vec_in, (per_frame(frame_shape, first), queries),
+                (smem(), info), frames_in(tokens, first), vec_in, frames_in(queries, first),
                 (whole(all_shape), key_rows), (whole(all_shape), value_rows), (whole((8, width)), class_own),
             ]
             + pair(space_w),
@@ -898,8 +1014,7 @@
                 low_out(frame_shape, first), low_out(mixed_shape, first), low_out(sprob_shape, first),
                 low_out(frame_shape, first), wide_out(frame_shape, first), sum_out,
             ],
-            space_held, flops=15 * square * count // own, nbytes=40 * row_bytes * count // own,
-            deps=deps, previous=kept,
+            space_held, micros=27 * count / own, deps=deps, previous=kept,
         )
         kept, class_own = tuple(outs[:-1]), outs[-1]
         if near is not None and first == 0:
@@ -916,9 +1031,9 @@
     class_row = jnp.broadcast_to(clip_class.astype(FLOAT), (8, width))
     small = whole((8, width))
     result, mlp_low, hidden, feed_grad, before_grad, rows_grad, mlp_sums = call(
-        functools.partial(mlp_kernel, places_here, frames), (own,),
+        functools.partial(mlp_kernel, places_here, frames), (own // group,),
         [
-            (smem(), info), (smem(), alive), (per_frame(frame_shape), places), (per_frame(frame_shape), grads),
+            (smem(), info), (smem(), alive), frames_in(places), frames_in(grads),
             (small, class_row), (small, class_own), (small, class_far), vec_in, (whole(bias.shape), bias),
         ]
         + pair(mlp_w),
@@ -926,8 +1041,8 @@
             low_out(frame_shape), low_out(frame_shape), low_out(hidden_shape), low_out(frame_shape),
             low_out(hidden_shape), wide_out(frame_shape), sum_out,
         ],
-        [pltpu.VMEM((wide // width, rows, width), FLOAT)] + mlp_held,
-        flops=30 * square, nbytes=40 * row_bytes,
+        [pltpu.VMEM((wide // width, group * rows, width), FLOAT)] + mlp_held,
+        micros=25,
     )
 
     mlp_mine, mlp_far = mlp_outer(my_slot, flat(mlp_low), flat(before_grad), flat(hidden), flat(feed_grad))
@@ -936,19 +1051,18 @@
 
     def space_back(first, count, sums, deps, previous):
         return call(
-            functools.partial(space_back_kernel, places_here, frames), (count,),
+            functools.partial(space_back_kernel, places_here, frames), (count // group,),
             [
-                (smem(), info), (per_frame(frame_shape, first), rows_grad), (class_spec, rows_grad),
-                (per_frame(frame_shape, first), after), (per_frame(mixed_shape, first), space_mixed),
-                (per_frame(sprob_shape, first), space_prob), vec_in, (small, sums),
+                (smem(), info), frames_in(rows_grad, first), (class_spec, rows_grad), frames_in(after, first),
+                frames_in(space_mixed, first), frames_in(space_prob, first), frames_in(space_att, first),
+                vec_in, (small, sums),
             ]
             + pair(space_w),
             [
                 low_out(frame_shape, first), low_out(mixed_shape, first), wide_out(frame_shape, first),
                 low_out(frame_shape, first), low_out(frame_shape, first), sum_out,
             ],
-            space_held, flops=20 * square * count // own, nbytes=40 * row_bytes * count // own,
-            deps=deps, previous=previous,
+            space_held, micros=30 * count / own, deps=deps, previous=previous,
         )
 
     half = own // 2
@@ -963,6 +1077,11 @@
         time_deps = []
     branch_grad, space_mixed_grad, after_grad, time_grad, time_att_grad, space_sums = outs
 
+    space_mine, space_far = space_outer(
+        my_slot, *[flat(v) for v in (space_low, space_mixed_grad, space_att, branch_grad, time_att, time_grad)],
+        deps=time_deps,
+    )
+    time_deps = time_deps + [space_far]
     far_frames = frames - own
     q_grad, own_grad, far_grad = call(
         time_back_kernel, (1,),
@@ -971,73 +1090,63 @@
             (whole(shape), sds(shape, BRAIN))
             for shape in (frame_shape, (2,) + frame_shape, (2, far_frames, rows, width))
         ],
-        flops=6 * square, nbytes=40 * row_bytes, deps=time_deps,
-    )
-    operands = [flat(v) for v in (space_low, space_mixed_grad, space_att, branch_grad, time_att, time_grad)]
+        micros=22, deps=time_deps,
+    )
     if near is not None:
         from_far = core_swap(far_grad)
-        mlp_parts = near.reduce_third(mlp_own, mlp_x, mlp_y, [q_grad])
-        mlp_first, mlp_second, mlp_others = mlp_parts
-        space_far = space_outer(far_slot, *operands, deps=[far_grad, mlp_second])
-        space_mine = space_outer(my_slot, *operands, deps=[space_far])
-        blocked = lambda v: v.reshape(BLOCKS, cut, v.shape[1])
-        space_a, space_b, space_x, space_y, space_own = near.reduce_first(
-            blocked(space_mine), core_swap(blocked(space_far)), [from_far]
-        )
+        mlp_first, mlp_second, mlp_others = near.reduce_third(mlp_own, mlp_x, mlp_y, [q_grad])
+        space_a, space_b, space_x, space_y, space_own = near.reduce_first(space_mine, core_swap(space_far), [mlp_second])
+        mixed_deps = [space_own]
     else:
+        mixed_deps = []
         padded = jnp.concatenate([jnp.zeros_like(own_grad), far_grad], axis=1)
         padded = jnp.roll(padded, core * own, axis=1)
         from_far = lax.psum_scatter(padded, "frame", scatter_dimension=1, tiled=True)
-        space_mine, space_far = space_outer(my_slot, *operands), space_outer(far_slot, *operands)
-    both = (own_grad.astype(FLOAT) + from_far.astype(FLOAT)).astype(BRAIN)
-    time_mixed_grad = jnp.concatenate([q_grad, both[0], both[1]], axis=-1)
+    pair_in = lambda v: (pl.BlockSpec((2, group, rows, width), lambda s: (0, s, 0, 0)), v)
+    time_mixed_grad = call(
+        mixed_grad_kernel, (own // group,), [frames_in(q_grad), pair_in(own_grad), pair_in(from_far)],
+        [low_out(mixed_shape)], micros=3, deps=mixed_deps,
+    )[0]
     outer = (flat(time_low), flat(time_mixed_grad))
 
-    back_deps = [] if near is None else [space_a, space_b]
+    back_deps = [] if near is None else [mlp_second, space_a, space_b]
     token_grad, time_sums = call(
-        time_mix_back_kernel, (own,),
-        [
-            (smem(), info), (per_frame(frame_shape), tokens), vec_in, (per_frame(mixed_shape), time_mixed_grad),
-            (per_frame(frame_shape), after_grad),
-        ]
+        time_mix_back_kernel, (own // group,),
+        [(smem(), info), frames_in(tokens), vec_in, frames_in(time_mixed_grad), frames_in(after_grad)]
         + pair(time_w),
         [wide_out(frame_shape), sum_out],
-        time_held, flops=3 * square, nbytes=30 * row_bytes, deps=back_deps,
+        time_held, micros=10, deps=back_deps,
     )
     bias_grad = mlp_sums[3 : 3 + bias_rows].reshape(width, bias_rows)
-    sums = jnp.concatenate([time_sums[:4], space_sums[5:6], space_sums[:5], mlp_sums[:3]], axis=0).T
-    n_sums = sums.shape[1]
-    blank = jnp.zeros((width, LANES - n_sums - bias_rows), FLOAT)
-    sums = jnp.concatenate([sums, bias_grad, blank], axis=1)
+    n_sums = 13
+    sums = call(
+        sums_kernel, (1,), [(small, time_sums), (small, space_sums), (small, mlp_sums), (whole(bias_grad.shape), bias_grad)],
+        [(whole((width, LANES)), sds((width, LANES), FLOAT))], [pltpu.VMEM((LANES, width), FLOAT)],
+    )[0]
 
     if near is not None:
-        mlp_grads = near.reduce_direct(mlp_first, mlp_second, mlp_others)
         space_x, space_y = near.reduce_second(space_x, space_y, space_a, space_b, [token_grad])
-        time_far = time_outer(far_slot, *outer, sums, deps=[space_x, space_y])
-        time_mine = time_outer(my_slot, *outer, sums, deps=[time_far])
-        space_parts = near.reduce_third(space_own, space_x, space_y, [time_mine])
-        time_a, time_b, time_x, time_y, time_own = near.reduce_first(
-            blocked(time_mine), core_swap(blocked(time_far)), []
-        )
+        time_mine, time_far = time_outer(my_slot, *outer, sums, deps=[space_x, space_y])
+        mlp_grads = near.reduce_direct(gate(mlp_first, [token_grad]), mlp_second, mlp_others)
+        time_a, time_b, time_x, time_y, time_own = near.reduce_first(time_mine, core_swap(time_far), [])
+        space_parts = near.reduce_third(space_own, space_x, space_y, [time_own])
         time_x, time_y = near.reduce_second(time_x, time_y, time_a, time_b, [space_parts[1]])
         time_parts = near.reduce_third(time_own, time_x, time_y, [])
-        grad_space = near.owner_rows(near.reduce_direct(*space_parts))
+        grad_space = near.reduce_direct(*space_parts)
         total = near.reduce_direct(*time_parts)
-        half = 3 * width // 2
-        grad_time = near.owner_rows(total[:, :half])
-        step = cut // 2
-        sums = lax.dynamic_slice_in_dim(total[:, half:], core * step, step, 0)
+        grad_time, sums = total[:, : 3 * width], total[:, 3 * width :]
         grad_mlp_down = mlp_grads[2 * cut :]
         grad_mlp_up = near.owner_rows(jnp.concatenate([mlp_grads[:cut], mlp_grads[cut : 2 * cut]], axis=1))
         class_total = space_sums[6:7] + core_swap(space_sums)[6:7]
     else:
         send = lambda v: lax.psum_scatter(v, AXES, scatter_dimension=0, tiled=True).astype(FLOAT)
-        time_mine, time_far = (time_outer(slot, *outer, sums)[:, : 3 * width // 2] for slot in (my_slot, far_slot))
+        spread = lambda mine, far: jnp.stack([mine, far], axis=1).reshape(width, mine.shape[2])
+        time_mine, time_far = time_outer(my_slot, *outer, sums)
         up = jnp.stack([v[:, : 2 * cut].reshape(BLOCKS, 2, cut, width) for v in (mlp_mine, mlp_far)])
         grad_mlp_up = send(jnp.transpose(up, (1, 3, 0, 2, 4)).reshape(width, wide))
         grad_mlp_down = send(jnp.stack([v[:, 2 * cut :] for v in (mlp_mine, mlp_far)], axis=1).reshape(wide, width))
-        grad_space = send(jnp.concatenate([space_mine, space_far], axis=1))
-        grad_time = send(jnp.concatenate([time_mine, time_far], axis=1))
+        grad_space = send(spread(space_mine, space_far))
+        grad_time = send(spread(time_mine, time_far)[:, : 3 * width])
         class_total = lax.psum(space_sums[6:7], "frame")
         step = width // (clips * cores)
         sums = lax.dynamic_slice_in_dim(lax.psum(sums, AXES), shard * step, step, 0)

time: 487 us -> 430 us (0.88)
  Pallas kernels: 261 us -> 239 us
  waiting for transfers between devices: 86 us -> 70.8 us
  other arithmetic: 18.9 us -> 8.64 us
  local copies, waits for them, and re-layouts: 49.4 us -> 43.5 us
    pallas_call x31 -> x34, Pallas kernels: 261 us -> 239 us  [call(): pl.pallas_call(inner, **common)]
    ppermute x42, waiting for transfers between devices: 70.1 us -> 61.4 us  [clip_swap(): return lax.ppermute(values, 'clip', [(i, i ^ bits) for i in range(count)])]
    ppermute x14 -> x12, waiting for transfers between devices: 15.9 us -> 9.38 us  [core_swap(): return lax.ppermute(values, 'frame', [(0, 1), (1, 0)])]
    slice x11 -> x1, local copies, waits for them, and re-layouts: 7.01 us -> 0.7 us  [body(): grad_time, sums = (total[:, :3 * width], total[:, 3 * width:])]
    concatenate x4 -> x0, other arithmetic: 5.27 us -> none  [the longest x2 4.33 us: body(): time_mixed_grad = jnp.concatenate([q_grad, both[0], both[1]], axis=-1)]
    unnamed x124 -> x114, local copies, waits for them, and re-layouts: 29.6 us -> 27.8 us
  transfers between devices with their start and end apart: 56 -> 54, of which waited for: 26 -> 21; matrix products, arithmetic and copies ran while one was open for 8% -> 6% of each run, Pallas kernels for 38% -> 40%
where the time goes in v1:
time: 430 us; the launch traced here: 424 us
  Pallas kernels  239 us (56%)
  waiting for transfers between devices  70.8 us (16%)
  starting transfers between devices  60.1 us (14%)
  local copies, waits for them, and re-layouts  43.5 us (10%)
  other arithmetic  8.64 us (2%)
    pallas_call x34, Pallas kernels, call(): pl.pallas_call(inner, **common)  239 us
    ppermute x42, waiting for transfers between devices, clip_swap(): return lax.ppermute(values, 'clip', [(i, i ^ bits) for i in range(count)])  61.4 us
    ppermute x42, starting transfers between devices, clip_swap(): return lax.ppermute(values, 'clip', [(i, i ^ bits) for i in range(count)])  57.7 us
    unnamed x114, local copies, waits for them, and re-layouts  27.8 us
    ppermute x12, waiting for transfers between devices, core_swap(): return lax.ppermute(values, 'frame', [(0, 1), (1, 0)])  9.38 us
  transfers between devices with their start and end apart: 54, of which 21 were waited for; matrix products, arithmetic and copies ran while one was open for 6% of the time, Pallas kernels for 40%

profile of v1, /device:TPU:0, one launch (start us, length us, event | category | flops | bytes accessed | tf_op | source)
XLA Modules:
  0.0 424.4 jit_solution(12936053327394594556)
XLA Ops:
  18.7 7.1 %collective-permute-done.2.refs_2_ = bf16[48,1280]{1,0:T(8,128)(2,1)S(1)} collective-permute-done((bf16[48,1280]{1,0:T(8,128)(2,1)}, bf16[48,1280]{1,0:T(8,128)(2,1)S(1)}, u32[]{:S(2)}, u32[]{:S(2)}) %collective-permute-start.2) | collective-permute-done | bytes 122912 | tf_op jit(solution)/shard_map/ppermute | solution.py:753
  66.2 12.5 %time_mix_kernel.1 = (bf16[4,208,768]{2,1,0:T(8,128)(2,1)}, bf16[8,208,768]{2,1,0:T(8,128)(2,1)}, bf16[8,208,768]{2,1,0:T(8,128)(2,1)}, bf16[4,208,768]{2,1,0:T(8,128)(2,1)}) custom-call(s32[5]{0:T(128)} %stack.27.refs_0_, bf16[8,208,768]{2,1,0:T(8,128)(2,1)} %pad_maximum_fusion.refs_7_.refs_1_, f32[128,768]{1,0:T(8,128)} %turn_kernel.1.refs_2_.refs_7_, ...), custom_call_target="tpu_custom_call" | custom-call | flops 12000000000 | bytes 1 | tf_op jit(solution)/shard_map/time_mix_kernel/pallas_call | solution.py:566
  78.7 5.0 %collective-permute-done.16.refs_2_ = bf16[192,768]{1,0:T(8,128)(2,1)S(1)} collective-permute-done((bf16[192,768]{1,0:T(8,128)(2,1)}, bf16[192,768]{1,0:T(8,128)(2,1)S(1)}, u32[]{:S(2)}, u32[]{:S(2)}) %collective-permute-start.16) | collective-permute-done | bytes 294944 | tf_op jit(solution)/shard_map/ppermute | solution.py:753
  91.7 8.2 %collective-permute-done.18.refs_4_ = bf16[2,48,1920]{2,1,0:T(8,128)(2,1)S(1)} collective-permute-done((bf16[2,48,1920]{2,1,0:T(8,128)(2,1)}, bf16[2,48,1920]{2,1,0:T(8,128)(2,1)S(1)}, u32[]{:S(2)}, u32[]{:S(2)}) %collective-permute-start.18) | collective-permute-done | bytes 368672 | tf_op jit(solution)/shard_map/ppermute | solution.py:753
  111.3 12.8 %attention_kernel.2 = (bf16[4,8,208,128]{3,2,1,0:T(8,128)(2,1)}, bf16[4,208,768]{2,1,0:T(8,128)(2,1)}, f32[4,208,768]{2,1,0:T(8,128)}, bf16[4,208,768]{2,1,0:T(8...) custom-call(s32[5]{0:T(128)} %stack.27.refs_0_, ...), custom_call_target="tpu_custom_call" | custom-call | flops 13500000256 | bytes 1 | tf_op jit(solution)/shard_map/attention_kernel/pallas_call | solution.py:566
  124.1 9.4 %collective-permute-done.21.refs_0_.refs_2_ = bf16[4,192,768]{2,1,0:T(8,128)(2,1)S(1)} collective-permute-done((bf16[4,192,768]{2,1,0:T(8,128)(2,1)}, bf16[4,192,768]{2,1,0:T(8,128)(2,1)S(1)}, u32[]{:S(2)}, u32[]{:S(2)}) %collective-permute-start.21) | collective-permute-done | bytes 1179680 | tf_op jit(solution)/shard_map/ppermute | solution.py:753
  139.7 13.3 %attention_kernel.3 = (bf16[4,8,208,128]{3,2,1,0:T(8,128)(2,1)}, bf16[4,208,768]{2,1,0:T(8,128)(2,1)}, f32[4,208,768]{2,1,0:T(8,128)}, bf16[4,208,768]{2,1,0:T(8...) custom-call(s32[5]{0:T(128)} %stack.27.refs_0_, ...), custom_call_target="tpu_custom_call", output_to_operand_aliasing={{0}: (9, {}), {1}: (10, {}), {2}: (11, {}), {3}: (12, {}), ... | custom-call | flops 13500000256 | bytes 1 | tf_op jit(solution)/shard_map/attention_kernel/pallas_call | solution.py:566
  154.1 4.8 %assemble_kernel.5.refs_9_ = bf16[16,192,768]{2,1,0:T(8,128)(2,1)} custom-call(s32[5]{0:T(128)} %stack.27.refs_0_, bf16[4,192,768]{2,1,0:T(8,128)(2,1)} %shard_map.261.refs_9_.refs_1_, bf16[4,192,768]{2,1,0:T(8,128)(2,1)} %copy-done.7, bf16[4,192,768]{2,1,0:T(8,128)(2,1)} %copy-done.8, bf16[2,192,768]{2,1,0:T(8,128)(2,1)} %copy-done.11, ...), custom_call_target="tpu_custom_call" | custom-call | flops 3000000000 | bytes 1 | tf_op jit(solution)/shard_map/assemble_kernel/pallas_call | solution.py:566
  162.0 4.9 %collective-permute-done.23.refs_6_ = f32[8,768]{1,0:T(8,128)S(1)} collective-permute-done((f32[8,768]{1,0:T(8,128)S(1)}, f32[8,768]{1,0:T(8,128)S(1)}, u32[]{:S(2)}, u32[]{:S(2)}) %collective-permute-start.23) | collective-permute-done | bytes 24608 | tf_op jit(solution)/shard_map/ppermute | solution.py:757
  167.7 25.5 %mlp_kernel.1 = (bf16[4,208,768]{2,1,0:T(8,128)(2,1)}, bf16[4,208,768]{2,1,0:T(8,128)(2,1)}, bf16[4,208,3072]{2,1,0:T(8,128)(2,1)}, bf16[4,208,768]{2,1,0:T(8,12...) custom-call(s32[5]{0:T(128)} %stack.27.refs_0_, ...), custom_call_target="tpu_custom_call" | custom-call | flops 24999999488 | bytes 1 | tf_op jit(solution)/shard_map/mlp_kernel/pallas_call | solution.py:566
  193.3 16.0 %mlp_outer_kernel.1 = (bf16[16,192,768]{2,1,0:T(8,128)(2,1)}, bf16[16,192,768]{2,1,0:T(8,128)(2,1)}) custom-call(s32[1]{0:T(128)} %bitcast.refs_0_, bf16[832,768]{1,0:T(8,128)(2,1)} %bitcast.84, bf16[832,3072]{1,0:T(8,128)(2,1)} %bitcast.72, bf16[832,3072]{1,0:T(8,128)(2,1)} %bitcast.71, bf16[832,768]{1,0:T(8,128)(2,1)} %bitcast.85), custom_call_target="tpu_custom_call" | custom-call | flops 20999999488 | bytes 1 | tf_op jit(solution)/shard_map/mlp_outer_kernel/pallas_call | solution.py:566
  211.8 16.2 %space_back_kernel.2 = (bf16[4,208,768]{2,1,0:T(8,128)(2,1)}, bf16[4,208,2304]{2,1,0:T(8,128)(2,1)}, f32[4,208,768]{2,1,0:T(8,128)}, bf16[4,208,768]{2,1,0:T(8,1...) custom-call(s32[5]{0:T(128)} %stack.27.refs_0_, f32[4,208,768]{2,1,0:T(8,128)} %get-tuple-element.134.refs_1_.refs_2_, ...), custom_call_target="tpu_custom_call" | custom-call | flops 15000000512 | bytes 1 | tf_op jit(solution)/shard_map/space_back_kernel/pallas_call | solution.py:566
  228.1 6.9 %reduce_first_kernel.3 = (bf16[2,192,768]{2,1,0:T(8,128)(2,1)}, bf16[2,192,768]{2,1,0:T(8,128)(2,1)}, bf16[4,192,768]{2,1,0:T(8,128)(2,1)}, bf16[4,192,768]{2,1,0:T(8,128)(2,1)}, bf16[4,192,768]{2,1,0:T(8,128)(2,1)}) custom-call(s32[5]{0:T(128)} %stack.27.refs_0_, bf16[4,4,192,768]{3,2,1,0:T(8,128)(2,1)} %bitcast.73, ...), custom_call_target="tpu_custom_call" | custom-call | flops 20000000000 | bytes 1 | tf_op jit(solution)/shard_map/reduce_first_kernel/pallas_call | solution.py:566
  237.1 16.3 %space_back_kernel.3 = (bf16[4,208,768]{2,1,0:T(8,128)(2,1)}, bf16[4,208,2304]{2,1,0:T(8,128)(2,1)}, f32[4,208,768]{2,1,0:T(8,128)}, bf16[4,208,768]{2,1,0:T(8,1...) custom-call(s32[5]{0:T(128)} %stack.27.refs_0_, ...), custom_call_target="tpu_custom_call", output_to_operand_aliasing={{0}: (11, {}), {1}: (12, {}), {2}: (13, {}), {3}: (14, {}),... | custom-call | flops 15000000512 | bytes 1 | tf_op jit(solution)/shard_map/space_back_kernel/pallas_call | solution.py:566
  260.8 12.0 %space_outer_kernel.1 = (bf16[16,24,3840]{2,1,0:T(8,128)(2,1)}, bf16[16,24,3840]{2,1,0:T(8,128)(2,1)}) custom-call(s32[1]{0:T(128)} %bitcast.refs_0_, bf16[832,768]{1,0:T(8,128)(2,1)} %bitcast.82, bf16[832,2304]{1,0:T(8,128)(2,1)} %bitcast.75, bf16[832,768]{1,0:T(8,128)(2,1)} %bitcast.83, bf16[832,768]{1,0:T(8,128)(2,1)} %bitcast.79, ...), custom_call_target="tpu_custom_call" | custom-call | flops 12000000000 | bytes 1 | tf_op jit(solution)/shard_map/space_outer_kernel/pallas_call | solution.py:566
  272.8 22.8 %time_back_kernel.1 = (bf16[4,208,768]{2,1,0:T(8,128)(2,1)}, bf16[2,4,208,768]{3,2,1,0:T(8,128)(2,1)}, bf16[2,4,208,768]{3,2,1,0:T(8,128)(2,1)}) custom-call(bf16[4,208,768]{2,1,0:T(8,128)(2,1)} %get-tuple-element.114.refs_4_.refs_2_.refs_3_.refs_0_, bf16[8,208,768]{2,1,0:T(8,128)(2,1)} %get-tuple-element.115.refs_4_.refs_1_, ...), custom_call_target="tpu_custom_call" | custom-call | flops 22000001024 | bytes 1 | tf_op jit(solution)/shard_map/time_back_kernel/pallas_call | solution.py:566
  302.0 6.9 %collective-permute-start.51 = (bf16[192,768]{1,0:T(8,128)(2,1)S(1)}, bf16[192,768]{1,0:T(8,128)(2,1)S(1)}, u32[]{:S(2)}, u32[]{:S(2)}) collective-permute-start(bf16[192,768]{1,0:T(8,128)(2,1)S(1)} %get-tuple-element.230), channel_id=1, source_target_pairs={{0,16},{2,18},{4,20},{6,22},{8,24},{10,26},{12,28},{14,30},{16,0},... | collective-permute-start | bytes 884744 | tf_op jit(solution)/shard_map/ppermute | solution.py:753
  310.5 5.0 %reduce_first_kernel.4 = (bf16[2,24,3840]{2,1,0:T(8,128)(2,1)}, bf16[2,24,3840]{2,1,0:T(8,128)(2,1)}, bf16[4,24,3840]{2,1,0:T(8,128)(2,1)}, bf16[4,24,3840]{2,1,0:T(8,128)(2,1)}, bf16[4,24,3840]{2,1,0:T(8,128)(2,1)}) custom-call(s32[5]{0:T(128)} %stack.27.refs_0_, bf16[4,4,24,3840]{3,2,1,0:T(8,128)(2,1)} %bitcast.76, bf16[4,4,24,3840]{3,2,1,0:T(8,128)(2,1)} %bitcast.69, ...), custom_call_target="tpu_custom_call" | custom-call | flops 20000000000 | bytes 1 | tf_op jit(solution)/shard_map/reduce_first_kernel/pallas_call | solution.py:566
  317.6 4.5 %mixed_grad_kernel.1.refs_3_ = bf16[4,208,2304]{2,1,0:T(8,128)(2,1)} custom-call(bf16[4,208,768]{2,1,0:T(8,128)(2,1)} %get-tuple-element.164.refs_4_.refs_0_, bf16[2,4,208,768]{3,2,1,0:T(8,128)(2,1)} %get-tuple-element.165.refs_1_, bf16[2,4,208,768]{3,2,1,0:T(8,128)(2,1)} %collective-permute-done.30.refs_2_, ...), custom_call_target="tpu_custom_call" | custom-call | flops 3000000000 | bytes 1 | tf_op jit(solution)/shard_map/mixed_grad_kernel/pallas_call | solution.py:566
  322.1 10.8 %time_mix_back_kernel.1 = (f32[4,208,768]{2,1,0:T(8,128)}, f32[8,768]{1,0:T(8,128)}) custom-call(s32[5]{0:T(128)} %stack.27.refs_0_, bf16[4,208,768]{2,1,0:T(8,128)(2,1)} %copy-done.1, f32[128,768]{1,0:T(8,128)} %turn_kernel.1.refs_2_.refs_7_, bf16[4,208,2304]{2,1,0:T(8,128)(2,1)} %mixed_grad_kernel.1.refs_3_, f32[4,208,768]{2,1,0:T(8,128)} %get-tuple-element.171.refs_4_, ...), custom_call_target="tpu_custom_call" | custom-call | flops 10000000000 | bytes 1 | tf_op jit(solution)/shard_map/time_mix_back_kernel/pallas_call | solution.py:566
  342.0 8.1 %time_outer_kernel.1 = (bf16[16,24,2432]{2,1,0:T(8,128)(2,1)}, bf16[16,24,2432]{2,1,0:T(8,128)(2,1)}) custom-call(s32[1]{0:T(128)} %bitcast.refs_0_, bf16[832,768]{1,0:T(8,128)(2,1)} %bitcast.78, bf16[832,2304]{1,0:T(8,128)(2,1)} %bitcast.74, f32[768,128]{1,0:T(8,128)} %sums_kernel.1.refs_3_, bf16[4,24,3840]{2,1,0:T(8,128)(2,1)} %get-tuple-element.181.refs_4_, ...), custom_call_target="tpu_custom_call" | custom-call | flops 8000000000 | bytes 1 | tf_op jit(solution)/shard_map/time_outer_kernel/pallas_call | solution.py:566
  369.9 9.6 %collective-permute-done.40.refs_2_ = bf16[4,24,3840]{2,1,0:T(8,128)(2,1)S(1)} collective-permute-done((bf16[4,24,3840]{2,1,0:T(8,128)(2,1)S(1)}, bf16[4,24,3840]{2,1,0:T(8,128)(2,1)S(1)}, u32[]{:S(2)}, u32[]{:S(2)}) %collective-permute-start.40) | collective-permute-done | bytes 737312 | tf_op jit(solution)/shard_map/ppermute | solution.py:753
  395.1 4.7 %collective-permute-done.48 = bf16[24,3840]{1,0:T(8,128)(2,1)S(1)} collective-permute-done((bf16[24,3840]{1,0:T(8,128)(2,1)S(1)}, bf16[24,3840]{1,0:T(8,128)(2,1)S(1)}, u32[]{:S(2)}, u32[]{:S(2)}) %collective-permute-start.48) | collective-permute-done | bytes 184352 | tf_op jit(solution)/shard_map/ppermute | solution.py:753
  413.4 5.0 %collective-permute-done.45 = bf16[24,2432]{1,0:T(8,128)(2,1)S(1)} collective-permute-done((bf16[24,2432]{1,0:T(8,128)(2,1)S(1)}, bf16[24,2432]{1,0:T(8,128)(2,1)S(1)}, u32[]{:S(2)}, u32[]{:S(2)}) %collective-permute-start.45) | collective-permute-done | bytes 116768 | tf_op jit(solution)/shard_map/ppermute | solution.py:753
  (278 shorter events, 173.7 us)
Async XLA Ops:
  18.7 33.2 %collective-permute-start.8 = (bf16[4,208,768]{2,1,0:T(8,128)(2,1)}, bf16[4,208,768]{2,1,0:T(8,128)(2,1)}, u32[]{:S(2)}, u32[]{:S(2)}) collective-permute-start(bf16[4,208,768]{2,1,0:T(8,128)(2,1)} %shard_map.257), channel_id=1, source_target_pairs={{0,1},{1,0},{2,3},{3,2},{4,5},{5,4},{6,7},{7,6},{8,9},{9,8},{10,11... | collective-permute-start | bytes 3833864 | tf_op jit(solution)/shard_map/ppermute | solution.py:757
  58.5 20.3 %collective-permute-start.15 = (bf16[192,768]{1,0:T(8,128)(2,1)}, bf16[192,768]{1,0:T(8,128)(2,1)S(1)}, u32[]{:S(2)}, u32[]{:S(2)}) collective-permute-start(bf16[192,768]{1,0:T(8,128)(2,1)} %shard_map.260.refs_6_.refs_0_), channel_id=1, source_target_pairs={{0,8},{2,10},{4,12},{6,14},{8,0},{10,2},{12,4},{14,6},{16,24},{18,... | collective-permute-start | bytes 884744 | tf_op jit(solution)/shard_map/ppermute | solution.py:753
  60.1 23.7 %collective-permute-start.16 = (bf16[192,768]{1,0:T(8,128)(2,1)}, bf16[192,768]{1,0:T(8,128)(2,1)S(1)}, u32[]{:S(2)}, u32[]{:S(2)}) collective-permute-start(bf16[192,768]{1,0:T(8,128)(2,1)} %shard_map.260.refs_6_.refs_0_), channel_id=1, source_target_pairs={{0,16},{2,18},{4,20},{6,22},{8,24},{10,26},{12,28},{14,30},{16,0},... | collective-permute-start | bytes 884744 | tf_op jit(solution)/shard_map/ppermute | solution.py:753
  61.2 22.6 %collective-permute-start.17 = (bf16[192,768]{1,0:T(8,128)(2,1)}, bf16[192,768]{1,0:T(8,128)(2,1)S(1)}, u32[]{:S(2)}, u32[]{:S(2)}) collective-permute-start(bf16[192,768]{1,0:T(8,128)(2,1)} %shard_map.260.refs_6_.refs_0_), channel_id=1, source_target_pairs={{0,24},{2,26},{4,28},{6,30},{8,16},{10,18},{12,20},{14,22},{16,8},... | collective-permute-start | bytes 884744 | tf_op jit(solution)/shard_map/ppermute | solution.py:753
  62.9 24.0 %collective-permute-start.13 = (bf16[4,48,1920]{2,1,0:T(8,128)(2,1)S(1)}, bf16[4,48,1920]{2,1,0:T(8,128)(2,1)S(1)}, u32[]{:S(2)}, u32[]{:S(2)}) collective-permute-start(bf16[4,48,1920]{2,1,0:T(8,128)(2,1)S(1)} %copy-done.9), channel_id=1, source_target_pairs={{0,2},{2,0},{4,6},{6,4},{8,10},{10,8},{12,14},{14,12},{16,18},{18,... | collective-permute-start | bytes 2211848 | tf_op jit(solution)/shard_map/ppermute | solution.py:753
  65.7 21.2 %collective-permute-start.14 = (bf16[4,48,1920]{2,1,0:T(8,128)(2,1)S(1)}, bf16[4,48,1920]{2,1,0:T(8,128)(2,1)S(1)}, u32[]{:S(2)}, u32[]{:S(2)}) collective-permute-start(bf16[4,48,1920]{2,1,0:T(8,128)(2,1)S(1)} %copy-done.10), channel_id=1, source_target_pairs={{0,4},{2,6},{4,0},{6,2},{8,12},{10,14},{12,8},{14,10},{16,20},{18,... | collective-permute-start | bytes 2211848 | tf_op jit(solution)/shard_map/ppermute | solution.py:753
  105.0 28.6 %collective-permute-start.21 = (bf16[4,192,768]{2,1,0:T(8,128)(2,1)}, bf16[4,192,768]{2,1,0:T(8,128)(2,1)S(1)}, u32[]{:S(2)}, u32[]{:S(2)}) collective-permute-start(bf16[4,192,768]{2,1,0:T(8,128)(2,1)} %shard_map.261.refs_9_.refs_1_), channel_id=1, source_target_pairs={{0,2},{2,0},{4,6},{6,4},{8,10},{10,8},{12,14},{14,12},{16,18},{18,... | collective-permute-start | bytes 3538952 | tf_op jit(solution)/shard_map/ppermute | solution.py:753
  105.5 28.3 %collective-permute-start.22 = (bf16[4,192,768]{2,1,0:T(8,128)(2,1)}, bf16[4,192,768]{2,1,0:T(8,128)(2,1)S(1)}, u32[]{:S(2)}, u32[]{:S(2)}) collective-permute-start(bf16[4,192,768]{2,1,0:T(8,128)(2,1)} %shard_map.261.refs_9_.refs_1_), channel_id=1, source_target_pairs={{0,4},{2,6},{4,0},{6,2},{8,12},{10,14},{12,8},{14,10},{16,20},{18,... | collective-permute-start | bytes 3538952 | tf_op jit(solution)/shard_map/ppermute | solution.py:753
  209.3 18.8 %collective-permute-start.27 = (bf16[16,192,768]{2,1,0:T(8,128)(2,1)}, bf16[16,192,768]{2,1,0:T(8,128)(2,1)}, u32[]{:S(2)}, u32[]{:S(2)}) collective-permute-start(bf16[16,192,768]{2,1,0:T(8,128)(2,1)} %get-tuple-element.143.refs_11_), channel_id=1, source_target_pairs={{0,1},{1,0},{2,3},{3,2},{4,5},{5,4},{6,7},{7,6},{8,9},{9,8},{10,11... | collective-permute-start | bytes 14155784 | tf_op jit(solution)/shard_map/ppermute | solution.py:757
  235.0 18.5 %collective-permute-start.28 = (bf16[2,192,768]{2,1,0:T(8,128)(2,1)}, bf16[2,192,768]{2,1,0:T(8,128)(2,1)S(1)}, u32[]{:S(2)}, u32[]{:S(2)}) collective-permute-start(bf16[2,192,768]{2,1,0:T(8,128)(2,1)} %get-tuple-element.151.refs_16_), channel_id=1, source_target_pairs={{0,4},{2,6},{4,0},{6,2},{8,12},{10,14},{12,8},{14,10},{16,20},{18,... | collective-permute-start | bytes 1769480 | tf_op jit(solution)/shard_map/ppermute | solution.py:753
  253.4 99.6 %collective-permute-start.34 = (f32[8,768]{1,0:T(8,128)}, f32[8,768]{1,0:T(8,128)S(1)}, u32[]{:S(2)}, u32[]{:S(2)}) collective-permute-start(f32[8,768]{1,0:T(8,128)} %get-tuple-element.175.refs_1_), channel_id=1, source_target_pairs={{0,1},{1,0},{2,3},{3,2},{4,5},{5,4},{6,7},{7,6},{8,9},{9,8},{10,11... | collective-permute-start | bytes 73736 | tf_op jit(solution)/shard_map/ppermute | solution.py:757
  258.8 37.3 %collective-permute-start.32 = (bf16[4,192,768]{2,1,0:T(8,128)(2,1)}, bf16[4,192,768]{2,1,0:T(8,128)(2,1)S(1)}, u32[]{:S(2)}, u32[]{:S(2)}) collective-permute-start(bf16[4,192,768]{2,1,0:T(8,128)(2,1)} %get-tuple-element.157.refs_7_.refs_5_), channel_id=1, source_target_pairs={{0,2},{2,0},{4,6},{6,4},{8,10},{10,8},{12,14},{14,12},{16,18},{18,... | collective-permute-start | bytes 3538952 | tf_op jit(solution)/shard_map/ppermute | solution.py:753
  259.8 36.3 %collective-permute-start.33 = (bf16[4,192,768]{2,1,0:T(8,128)(2,1)}, bf16[4,192,768]{2,1,0:T(8,128)(2,1)S(1)}, u32[]{:S(2)}, u32[]{:S(2)}) collective-permute-start(bf16[4,192,768]{2,1,0:T(8,128)(2,1)} %get-tuple-element.158.refs_8_.refs_6_), channel_id=1, source_target_pairs={{0,4},{2,6},{4,0},{6,2},{8,12},{10,14},{12,8},{14,10},{16,20},{18,... | collective-permute-start | bytes 3538952 | tf_op jit(solution)/shard_map/ppermute | solution.py:753
  272.8 36.1 %collective-permute-start.31 = (bf16[16,24,3840]{2,1,0:T(8,128)(2,1)}, bf16[16,24,3840]{2,1,0:T(8,128)(2,1)S(1)}, u32[]{:S(2)}, u32[]{:S(2)}) collective-permute-start(bf16[16,24,3840]{2,1,0:T(8,128)(2,1)} %get-tuple-element.163.refs_7_), channel_id=1, source_target_pairs={{0,1},{1,0},{2,3},{3,2},{4,5},{5,4},{6,7},{7,6},{8,9},{9,8},{10,11... | collective-permute-start | bytes 8847368 | tf_op jit(solution)/shard_map/ppermute | solution.py:757
  295.6 21.0 %collective-permute-start.30 = (bf16[2,4,208,768]{3,2,1,0:T(8,128)(2,1)}, bf16[2,4,208,768]{3,2,1,0:T(8,128)(2,1)}, u32[]{:S(2)}, u32[]{:S(2)}) collective-permute-start(bf16[2,4,208,768]{3,2,1,0:T(8,128)(2,1)} %get-tuple-element.166), channel_id=1, source_target_pairs={{0,1},{1,0},{2,3},{3,2},{4,5},{5,4},{6,7},{7,6},{8,9},{9,8},{10,11... | collective-permute-start | bytes 7667720 | tf_op jit(solution)/shard_map/ppermute | solution.py:757
  302.0 52.3 %collective-permute-start.51 = (bf16[192,768]{1,0:T(8,128)(2,1)S(1)}, bf16[192,768]{1,0:T(8,128)(2,1)S(1)}, u32[]{:S(2)}, u32[]{:S(2)}) collective-permute-start(bf16[192,768]{1,0:T(8,128)(2,1)S(1)} %get-tuple-element.230), channel_id=1, source_target_pairs={{0,16},{2,18},{4,20},{6,22},{8,24},{10,26},{12,28},{14,30},{16,0},... | collective-permute-start | bytes 884744 | tf_op jit(solution)/shard_map/ppermute | solution.py:753
  308.9 45.5 %collective-permute-start.50 = (bf16[192,768]{1,0:T(8,128)(2,1)}, bf16[192,768]{1,0:T(8,128)(2,1)S(1)}, u32[]{:S(2)}, u32[]{:S(2)}) collective-permute-start(bf16[192,768]{1,0:T(8,128)(2,1)} %get-tuple-element.169.refs_3_.refs_7_), channel_id=1, source_target_pairs={{0,8},{2,10},{4,12},{6,14},{8,0},{10,2},{12,4},{14,6},{16,24},{18,... | collective-permute-start | bytes 884744 | tf_op jit(solution)/shard_map/ppermute | solution.py:753
  315.5 19.6 %collective-permute-start.35 = (bf16[2,24,3840]{2,1,0:T(8,128)(2,1)}, bf16[2,24,3840]{2,1,0:T(8,128)(2,1)S(1)}, u32[]{:S(2)}, u32[]{:S(2)}) collective-permute-start(bf16[2,24,3840]{2,1,0:T(8,128)(2,1)} %get-tuple-element.172.refs_8_), channel_id=1, source_target_pairs={{0,4},{2,6},{4,0},{6,2},{8,12},{10,14},{12,8},{14,10},{16,20},{18,... | collective-permute-start | bytes 1105928 | tf_op jit(solution)/shard_map/ppermute | solution.py:753
  316.6 20.8 %collective-permute-start.36 = (bf16[2,24,3840]{2,1,0:T(8,128)(2,1)}, bf16[2,24,3840]{2,1,0:T(8,128)(2,1)S(1)}, u32[]{:S(2)}, u32[]{:S(2)}) collective-permute-start(bf16[2,24,3840]{2,1,0:T(8,128)(2,1)} %get-tuple-element.173.refs_9_), channel_id=1, source_target_pairs={{0,2},{2,0},{4,6},{6,4},{8,10},{10,8},{12,14},{14,12},{16,18},{18,... | collective-permute-start | bytes 1105928 | tf_op jit(solution)/shard_map/ppermute | solution.py:753
  335.1 19.2 %collective-permute-start.52 = (bf16[192,768]{1,0:T(8,128)(2,1)S(1)}, bf16[192,768]{1,0:T(8,128)(2,1)S(1)}, u32[]{:S(2)}, u32[]{:S(2)}) collective-permute-start(bf16[192,768]{1,0:T(8,128)(2,1)S(1)} %get-tuple-element.231), channel_id=1, source_target_pairs={{0,24},{2,26},{4,28},{6,30},{8,16},{10,18},{12,20},{14,22},{16,8},... | collective-permute-start | bytes 884744 | tf_op jit(solution)/shard_map/ppermute | solution.py:753
  360.3 19.3 %collective-permute-start.40 = (bf16[4,24,3840]{2,1,0:T(8,128)(2,1)S(1)}, bf16[4,24,3840]{2,1,0:T(8,128)(2,1)S(1)}, u32[]{:S(2)}, u32[]{:S(2)}) collective-permute-start(bf16[4,24,3840]{2,1,0:T(8,128)(2,1)S(1)} %copy-done.22), channel_id=1, source_target_pairs={{0,2},{2,0},{4,6},{6,4},{8,10},{10,8},{12,14},{14,12},{16,18},{18,... | collective-permute-start | bytes 2211848 | tf_op jit(solution)/shard_map/ppermute | solution.py:753
  361.3 19.3 %collective-permute-start.41 = (bf16[4,24,3840]{2,1,0:T(8,128)(2,1)S(1)}, bf16[4,24,3840]{2,1,0:T(8,128)(2,1)S(1)}, u32[]{:S(2)}, u32[]{:S(2)}) collective-permute-start(bf16[4,24,3840]{2,1,0:T(8,128)(2,1)S(1)} %copy-done.21), channel_id=1, source_target_pairs={{0,4},{2,6},{4,0},{6,2},{8,12},{10,14},{12,8},{14,10},{16,20},{18,... | collective-permute-start | bytes 2211848 | tf_op jit(solution)/shard_map/ppermute | solution.py:753
  367.8 20.8 %collective-permute-start.38 = (bf16[2,24,2432]{2,1,0:T(8,128)(2,1)}, bf16[2,24,2432]{2,1,0:T(8,128)(2,1)S(1)}, u32[]{:S(2)}, u32[]{:S(2)}) collective-permute-start(bf16[2,24,2432]{2,1,0:T(8,128)(2,1)} %get-tuple-element.188), channel_id=1, source_target_pairs={{0,4},{2,6},{4,0},{6,2},{8,12},{10,14},{12,8},{14,10},{16,20},{18,... | collective-permute-start | bytes 700424 | tf_op jit(solution)/shard_map/ppermute | solution.py:753
  368.9 19.8 %collective-permute-start.39 = (bf16[2,24,2432]{2,1,0:T(8,128)(2,1)}, bf16[2,24,2432]{2,1,0:T(8,128)(2,1)S(1)}, u32[]{:S(2)}, u32[]{:S(2)}) collective-permute-start(bf16[2,24,2432]{2,1,0:T(8,128)(2,1)} %get-tuple-element.189), channel_id=1, source_target_pairs={{0,2},{2,0},{4,6},{6,4},{8,10},{10,8},{12,14},{14,12},{16,18},{18,... | collective-permute-start | bytes 700424 | tf_op jit(solution)/shard_map/ppermute | solution.py:753
  (83 other events, 448.9 us)
